TPU v7x, 512 devices: a whole 4x8x8 slice. The times are simulated.
512 devices in a mesh: gx: 16 (over z, core), yz: 32 (over y, x).
Axes of the slice: x: 4, y: 8, z: 8, core: 2. Of those that a mesh axis runs over, the one named last changes fastest.
Arguments:
- classes: int32 [128, 128, 128], P('gx', 'yz'), may hold values from 0 to 3
- contrast: float32 [4], replicated, may hold values from 0.25 to 25
- shift_x: int32 [128, 128, 7], P('gx', 'yz'), may hold values from -3 to 3, as said below
- shift_y: int32 [128, 128, 7], P('gx', 'yz'), may hold values from -3 to 3, as said below
- extent: int32 [128, 128], P('gx', 'yz'), may hold values from 1 to 8
- coarse_basis: float32 [8, 128], replicated, may hold values from -4 to 4
- stiffness: float32 [1024, 1024], replicated, may hold values from -1 to 2, as said below
Outputs:
- correction: float32 [128, 128, 8, 128], P('gx', 'yz')
Inputs may be any that keep to these rules, and one draw needn't show every extreme that they name: `stiffness`: symmetric. For each element, the pairs (shift_x, shift_y) of its 7 slots are distinct positions of the box of reach 3, none of them (0, 0). `shift_y`: paired with shift_x as stated there.
All inputs are finite; a program needn't handle non-finite values.
Results may differ from a plain program's by a relative error of at most 0.0003.
Values sent between devices are 32-bit elements; how exact they have to be, the bound alone decides.
No kernel may reach another device: no remote copies, remote signals or barrier semaphores. Data moves between devices by JAX's collectives and lax.ppermute only.
A program may use at most 64 MiB of HBM per device.

v0:
```python
import jax
import jax.numpy as jnp
from jax import lax
from jax.sharding import PartitionSpec as P

SLOTS = 8
NGRP = 8
REACH = 3
NCLASS = 4
ITERS = 3


def padded(block, sides, width):
    for axis, dim in sides:
        count = lax.axis_size(axis)
        forward = [(i, i + 1) for i in range(count - 1)]
        forward.append((count - 1, 0))
        backward = [(target, source) for source, target in forward]
        low = lax.ppermute(
            lax.slice_in_dim(block, block.shape[dim] - width, None, axis=dim), axis, forward
        )
        high = lax.ppermute(lax.slice_in_dim(block, 0, width, axis=dim), axis, backward)
        block = jnp.concatenate([low, block, high], axis=dim)
    return block


def passed_along(value, axis, steps):
    count = lax.axis_size(axis)
    pairs = [(source, (source + steps) % count) for source in range(count)]
    return lax.ppermute(value, axis, pairs)


def coefficient_scale(classes, contrast):
    matches = classes[..., None] == jnp.arange(NCLASS, dtype=jnp.int32)
    return jnp.sqrt(jnp.sum(jnp.where(matches, contrast, jnp.zeros_like(contrast)), axis=-1))


def correct(slot_scale, active, coarse, stiffness, dof_count):
    patches, patch_order = slot_scale.shape
    columns = coarse.shape[0]
    group_size = dof_count // NGRP
    groups = patch_order // group_size

    def operate(vector):
        scaled = (slot_scale[:, None, :] * vector).reshape(patches * columns, patch_order)
        product = jnp.dot(
            scaled, stiffness, precision=lax.Precision.HIGHEST, preferred_element_type=jnp.float32
        )
        return (active * slot_scale)[:, None, :] * product.reshape(patches, columns, patch_order)

    forcing = -operate(jnp.broadcast_to(coarse, (patches, columns, patch_order)))
    inverse = 1.0 / (slot_scale * slot_scale)
    weight_sums = inverse.reshape(patches, groups, group_size).sum(-1)
    corrector = jnp.zeros_like(forcing)
    for iteration in range(ITERS):
        residual = forcing
        if iteration > 0:
            residual = forcing - operate(corrector)
        weighted = residual * inverse[:, None, :]
        multiplier = (
            weighted.reshape(patches, columns, groups, group_size).sum(-1) / weight_sums[:, None, :]
        )
        spread = jnp.repeat(multiplier, group_size, axis=-1)
        corrector = corrector + active[:, None, :] * (weighted - spread * inverse[:, None, :])
    return corrector


def per_device(classes, contrast, shift_x, shift_y, extent, coarse_basis, stiffness):
    row_count, col_count, dof_count = classes.shape
    columns = coarse_basis.shape[0]
    patch_order = SLOTS * dof_count
    patches = row_count * col_count
    coef_scale = coefficient_scale(classes, contrast)
    extended = padded(coef_scale, (("gx", 0), ("yz", 1)), REACH)
    ext_rows = row_count + 2 * REACH
    ext_cols = col_count + 2 * REACH
    grid_row = lax.broadcasted_iota(jnp.int32, (row_count, col_count, 1), 0)
    grid_col = lax.broadcasted_iota(jnp.int32, (row_count, col_count, 1), 1)
    index_x = jnp.concatenate([grid_row, grid_row + shift_x], axis=2) + REACH
    index_y = jnp.concatenate([grid_col, grid_col + shift_y], axis=2) + REACH
    flat_index = (index_x * ext_cols + index_y).reshape(-1)
    slot_scale = jnp.take(
        extended.reshape(ext_rows * ext_cols, dof_count), flat_index, axis=0
    ).reshape(patches, patch_order)
    live = jnp.arange(SLOTS, dtype=jnp.int32)[None, :] < extent.reshape(patches, 1)
    active = jnp.repeat(live.astype(jnp.float32), dof_count, axis=1)
    coarse = jnp.zeros((columns, patch_order), jnp.float32).at[:, :dof_count].set(coarse_basis)
    corrector = correct(slot_scale, active, coarse, stiffness, dof_count)
    values = (
        corrector.reshape(patches, columns, SLOTS, dof_count)
        .transpose(0, 2, 1, 3)
        .reshape(patches * SLOTS, columns, dof_count)
    )
    collected = (
        jnp.zeros((ext_rows * ext_cols, columns, dof_count), jnp.float32).at[flat_index].add(values)
    )
    collected = collected.reshape(ext_rows, ext_cols, columns, dof_count)
    starts_x = {-1: 0, 0: REACH, 1: REACH + row_count}
    sizes_x = {-1: REACH, 0: row_count, 1: REACH}
    places_x = {-1: row_count - REACH, 0: 0, 1: 0}
    starts_y = {-1: 0, 0: REACH, 1: REACH + col_count}
    sizes_y = {-1: REACH, 0: col_count, 1: REACH}
    places_y = {-1: col_count - REACH, 0: 0, 1: 0}
    summed = collected[REACH : REACH + row_count, REACH : REACH + col_count]
    for toward_x in (-1, 0, 1):
        for toward_y in (-1, 0, 1):
            if toward_x == 0 and toward_y == 0:
                continue
            first_x = starts_x[toward_x]
            first_y = starts_y[toward_y]
            length_x = sizes_x[toward_x]
            length_y = sizes_y[toward_y]
            pieces = collected[first_x : first_x + length_x, first_y : first_y + length_y]
            if toward_x != 0:
                pieces = passed_along(pieces, "gx", toward_x)
            if toward_y != 0:
                pieces = passed_along(pieces, "yz", toward_y)
            target_x = places_x[toward_x]
            target_y = places_y[toward_y]
            summed = summed.at[target_x : target_x + length_x, target_y : target_y + length_y].add(
                pieces
            )
    return summed


def solution(mesh):
    return jax.shard_map(
        per_device,
        mesh=mesh,
        in_specs=(
            P("gx", "yz", None),
            P(),
            P("gx", "yz", None),
            P("gx", "yz", None),
            P("gx", "yz"),
            P(),
            P(),
        ),
        out_specs=P("gx", "yz", None, None),
        check_vma=False,
    )
```

profile of v0, /device:TPU:32, one launch (start us, length us, event | category | flops | bytes accessed | tf_op | source)
XLA Modules:
  0.0 143.1 jit_solution(16304316831902351060)
XLA Ops:
  1.5 8.5 %collective-permute-start.1 = (f32[3,4,128]{2,0,1:T(4,128)S(1)}, f32[3,4,128]{2,0,1:T(4,128)S(1)}, u32[]{:S(2)}, u32[]{:S(2)}) collective-permute-start(f32[3,4,128]{2,0,1:T(4,128)S(1)} %get-tuple-element.130), channel_id=1, source_target_pairs={{32,0},{64,32},{96,64},{128,96},{160,128},{192,160},{224,192},{256... | collective-permute-start | bytes 18440 | tf_op jit(solution)/shard_map/ppermute | solution.py:22
  14.6 3.4 %collective-permute-start.2 = (f32[14,3,128]{2,0,1:T(8,128)S(1)}, f32[14,3,128]{2,0,1:T(8,128)S(1)}, u32[]{:S(2)}, u32[]{:S(2)}) collective-permute-start(f32[14,3,128]{2,0,1:T(8,128)S(1)} %get-tuple-element.127), channel_id=1, source_target_pairs={{0,1},{1,2},{2,3},{3,4},{4,5},{5,6},{6,7},{7,8},{8,9},{9,10},{10,1... | collective-permute-start | bytes 64520 | tf_op jit(solution)/shard_map/ppermute | solution.py:19
  18.0 5.8 %collective-permute-start.3 = (f32[14,3,128]{2,0,1:T(8,128)S(1)}, f32[14,3,128]{2,0,1:T(8,128)S(1)}, u32[]{:S(2)}, u32[]{:S(2)}) collective-permute-start(f32[14,3,128]{2,0,1:T(8,128)S(1)} %get-tuple-element.128), channel_id=1, source_target_pairs={{1,0},{2,1},{3,2},{4,3},{5,4},{6,5},{7,6},{8,7},{9,8},{10,9},{11,1... | collective-permute-start | bytes 64520 | tf_op jit(solution)/shard_map/ppermute | solution.py:22
  26.6 5.9 %broadcast_multiply_fusion = (f32[32,8,1024]{2,1,0:T(8,128)S(1)}, f32[32,8,1024]{2,1,0:T(8,128)S(1)}) fusion(f32[32,1024]{1,0:T(8,128)S(1)} %get-tuple-element.117, f32[1024,1024]{1,0:T(8,128)} %param.31, f32[8,1024]{1,0:T(8,128)} %scatter.4, f32[32,1024]{1,0:T(8,128)S(1)} %get-tuple-element.118, f32[32,1024]{1,0:T(8,128)S(1)} %fusion.46), kind=kOutput, calls=%fused_computation.27 | convolution fusion | flops 3222274048 | bytes 6717440 | tf_op jit(solution)/shard_map/dot_general | solution.py:46
  32.5 2.7 %copy.37 = f32[32,8,1024]{0,2,1:T(8,128)} copy(f32[32,8,1024]{2,1,0:T(8,128)S(1)} %get-tuple-element.133) | data formatting | bytes 2097152 | tf_op jit(solution)/shard_map/mul | solution.py:59
  35.2 3.1 %bitcast_reduce_fusion.2 = f32[32,8,64]{0,2,1:T(8,128)S(1)} fusion(f32[32,8,1024]{0,2,1:T(8,128)} %copy.37), kind=kLoop, calls=%fused_computation.4 | loop fusion | flops 245760 | bytes 1114112 | tf_op jit(solution)/shard_map/reduce_sum | solution.py:61
  41.5 3.0 %copy.41 = f32[32,8,1024]{2,1,0:T(8,128)S(1)} copy(f32[32,8,1024]{0,2,1:T(8,128)} %bitcast.56) | data formatting | bytes 2097152 | tf_op jit(solution)/shard_map/reshape | solution.py:63
  44.6 6.2 %fusion.27 = f32[32,8,1024]{2,1,0:T(8,128)S(1)} fusion(f32[32,8,1024]{2,1,0:T(8,128)S(1)} %get-tuple-element.134, f32[1024,1024]{1,0:T(8,128)} %param.31, f32[32,1024]{1,0:T(8,128)S(1)} %get-tuple-element.117, f32[32,1024]{1,0:T(8,128)S(1)} %get-tuple-element.118, f32[32,1024]{1,0:T(8,128)S(1)} %fusion.46, f32[32,8,1024]{2,1,0:T(8,128)S(1)} %copy.41, ...), kind=kOutput, calls=%fused_computation.18 | convolution fusion | flops 3223322624 | bytes 7864320 | tf_op jit(solution)/shard_map/dot_general | solution.py:46
  50.8 2.7 %copy.42 = f32[32,8,1024]{0,2,1:T(8,128)} copy(f32[32,8,1024]{2,1,0:T(8,128)S(1)} %fusion.27) | data formatting | bytes 2097152 | tf_op jit(solution)/shard_map/mul | solution.py:59
  53.5 3.1 %bitcast_reduce_fusion.1 = f32[32,8,64]{0,2,1:T(8,128)S(1)} fusion(f32[32,8,1024]{0,2,1:T(8,128)} %copy.42), kind=kLoop, calls=%fused_computation.3 | loop fusion | flops 245760 | bytes 1114112 | tf_op jit(solution)/shard_map/reduce_sum | solution.py:61
  56.6 2.2 %broadcast_in_dim.76 = f32[32,8,64,16]{0,3,2,1:T(8,128)} broadcast(f32[32,8,64]{0,2,1:T(8,128)S(1)} %broadcast_divide_fusion.1), dimensions={0,1,2} | broadcast | bytes 1114112 | tf_op jit(solution)/shard_map/broadcast_in_dim | solution.py:63
  58.9 3.7 %copy.43 = f32[32,8,1024]{2,1,0:T(8,128)} copy(f32[32,8,1024]{0,2,1:T(8,128)} %bitcast.57) | data formatting | bytes 2097152 | tf_op jit(solution)/shard_map/reshape | solution.py:63
  62.6 7.5 %fusion.24 = f32[32,8,1024]{2,1,0:T(8,128)} fusion(f32[32,8,1024]{2,1,0:T(8,128)S(1)} %get-tuple-element.134, f32[1024,1024]{1,0:T(8,128)} %param.31, f32[32,1024]{1,0:T(8,128)S(1)} %get-tuple-element.117, f32[32,1024]{1,0:T(8,128)S(1)} %get-tuple-element.118, f32[32,1024]{1,0:T(8,128)S(1)} %fusion.46, f32[32,8,1024]{2,1,0:T(8,128)S(1)} %fusion.27, ...), kind=kOutput, calls=%fused_computation.17 | convolution fusion | flops 3224371200 | bytes 9961472 | tf_op jit(solution)/shard_map/dot_general | solution.py:46
  70.2 3.7 %copy.44 = f32[32,8,1024]{0,2,1:T(8,128)} copy(f32[32,8,1024]{2,1,0:T(8,128)} %fusion.24) | data formatting | bytes 2097152 | tf_op jit(solution)/shard_map/mul | solution.py:59
  73.8 3.1 %bitcast_reduce_fusion = f32[32,8,64]{0,2,1:T(8,128)S(1)} fusion(f32[32,8,1024]{0,2,1:T(8,128)} %copy.44), kind=kLoop, calls=%fused_computation.2 | loop fusion | flops 245760 | bytes 1114112 | tf_op jit(solution)/shard_map/reduce_sum | solution.py:61
  79.3 3.7 %copy.45 = f32[32,8,1024]{2,1,0:T(8,128)} copy(f32[32,8,1024]{0,2,1:T(8,128)} %bitcast.58) | data formatting | bytes 2097152 | tf_op jit(solution)/shard_map/reshape | solution.py:63
  83.0 3.7 %multiply_add_fusion = f32[32,8,1024]{2,1,0:T(8,128)} fusion(f32[32,8,1024]{2,1,0:T(8,128)} %fusion.24, f32[32,8,1024]{2,1,0:T(8,128)} %copy.45, f32[32,1024]{1,0:T(8,128)S(1)} %get-tuple-element.117, f32[32,1024]{1,0:T(8,128)S(1)} %bitcast.67, f32[32,8,1024]{2,1,0:T(8,128)S(1)} %fusion.27, f32[32,8,1024]{2,1,0:T(8,128)} %copy.43, ...), kind=kLoop, calls=%fused_computation.19 | loop fusion | flops 3145728 | bytes 7602176 | tf_op jit(solution)/shard_map/add | solution.py:64
  86.7 18.2 %scatter_fusion = f32[140,8,128]{2,1,0:T(8,128)S(1)} fusion(f32[140,8,128]{2,1,0:T(8,128)S(1)} %broadcast_in_dim.63, s32[256]{0:T(256)S(1)} %bitcast.73, f32[256,8,128]{2,1,0:T(8,128)} %bitcast.64), kind=kCustom, calls=%fused_computation.1 | custom fusion | flops 262144 | bytes 3146752 | tf_op jit(solution)/shard_map/scatter-add | solution.py:95
  106.7 7.4 %collective-permute-start.5 = (f32[3,3,8,128]{3,2,1,0:T(8,128)S(1)}, f32[3,3,8,128]{3,2,1,0:T(8,128)S(1)}, u32[]{:S(2)}, u32[]{:S(2)}) collective-permute-start(f32[3,3,8,128]{3,2,1,0:T(8,128)S(1)} %collective-permute-done.4), channel_id=1, source_target_pairs={{0,31},{1,0},{2,1},{3,2},{4,3},{5,4},{6,5},{7,6},{8,7},{9,8},{10,9... | collective-permute-start | bytes 110600 | tf_op jit(solution)/shard_map/ppermute | solution.py:30
  114.1 2.7 %collective-permute-start.6 = (f32[3,4,8,128]{3,2,1,0:T(8,128)S(1)}, f32[3,4,8,128]{3,2,1,0:T(8,128)S(1)}, u32[]{:S(2)}, u32[]{:S(2)}) collective-permute-start(f32[3,4,8,128]{3,2,1,0:T(8,128)S(1)} %get-tuple-element.124), channel_id=1, source_target_pairs={{0,480},{32,0},{64,32},{96,64},{128,96},{160,128},{192,160},{224,1... | collective-permute-start | bytes 147464 | tf_op jit(solution)/shard_map/ppermute | solution.py:30
  119.1 3.6 %collective-permute-start.10 = (f32[8,3,8,128]{3,2,1,0:T(8,128)S(1)}, f32[8,3,8,128]{3,2,1,0:T(8,128)S(1)}, u32[]{:S(2)}, u32[]{:S(2)}) collective-permute-start(f32[8,3,8,128]{3,2,1,0:T(8,128)S(1)} %get-tuple-element.125), channel_id=1, source_target_pairs={{0,1},{1,2},{2,3},{3,4},{4,5},{5,6},{6,7},{7,8},{8,9},{9,10},{10,1... | collective-permute-start | bytes 294920 | tf_op jit(solution)/shard_map/ppermute | solution.py:30
  124.9 2.4 %collective-permute-done.11 = f32[3,3,8,128]{3,2,1,0:T(8,128)S(1)} collective-permute-done((f32[3,3,8,128]{3,2,1,0:T(8,128)S(1)}, f32[3,3,8,128]{3,2,1,0:T(8,128)S(1)}, u32[]{:S(2)}, u32[]{:S(2)}) %collective-permute-start.11) | collective-permute-done | bytes 36896 | tf_op jit(solution)/shard_map/ppermute | solution.py:30
  127.7 5.5 %collective-permute-start.12 = (f32[3,3,8,128]{3,2,1,0:T(8,128)S(1)}, f32[3,3,8,128]{3,2,1,0:T(8,128)S(1)}, u32[]{:S(2)}, u32[]{:S(2)}) collective-permute-start(f32[3,3,8,128]{3,2,1,0:T(8,128)S(1)} %collective-permute-done.11), channel_id=1, source_target_pairs={{0,31},{1,0},{2,1},{3,2},{4,3},{5,4},{6,5},{7,6},{8,7},{9,8},{10,9... | collective-permute-start | bytes 110600 | tf_op jit(solution)/shard_map/ppermute | solution.py:30
  136.6 5.9 %collective-permute-done.15 = f32[3,3,8,128]{3,2,1,0:T(8,128)S(1)} collective-permute-done((f32[3,3,8,128]{3,2,1,0:T(8,128)S(1)}, f32[3,3,8,128]{3,2,1,0:T(8,128)S(1)}, u32[]{:S(2)}, u32[]{:S(2)}) %collective-permute-start.15) | collective-permute-done | bytes 36896 | tf_op jit(solution)/shard_map/ppermute | solution.py:30
  (90 shorter events, 24.7 us)
Async XLA Ops:
  1.5 13.1 %collective-permute-start = (f32[3,4,128]{2,0,1:T(4,128)S(1)}, f32[3,4,128]{2,0,1:T(4,128)S(1)}, u32[]{:S(2)}, u32[]{:S(2)}) collective-permute-start(f32[3,4,128]{2,0,1:T(4,128)S(1)} %get-tuple-element.129), channel_id=1, source_target_pairs={{0,32},{32,64},{64,96},{96,128},{128,160},{160,192},{192,224},{224... | collective-permute-start | bytes 18440 | tf_op jit(solution)/shard_map/ppermute | solution.py:19
  1.5 13.1 %collective-permute-start.1 = (f32[3,4,128]{2,0,1:T(4,128)S(1)}, f32[3,4,128]{2,0,1:T(4,128)S(1)}, u32[]{:S(2)}, u32[]{:S(2)}) collective-permute-start(f32[3,4,128]{2,0,1:T(4,128)S(1)} %get-tuple-element.130), channel_id=1, source_target_pairs={{32,0},{64,32},{96,64},{128,96},{160,128},{192,160},{224,192},{256... | collective-permute-start | bytes 18440 | tf_op jit(solution)/shard_map/ppermute | solution.py:22
  14.6 10.7 %collective-permute-start.2 = (f32[14,3,128]{2,0,1:T(8,128)S(1)}, f32[14,3,128]{2,0,1:T(8,128)S(1)}, u32[]{:S(2)}, u32[]{:S(2)}) collective-permute-start(f32[14,3,128]{2,0,1:T(8,128)S(1)} %get-tuple-element.127), channel_id=1, source_target_pairs={{0,1},{1,2},{2,3},{3,4},{4,5},{5,6},{6,7},{7,8},{8,9},{9,10},{10,1... | collective-permute-start | bytes 64520 | tf_op jit(solution)/shard_map/ppermute | solution.py:19
  18.0 7.3 %collective-permute-start.3 = (f32[14,3,128]{2,0,1:T(8,128)S(1)}, f32[14,3,128]{2,0,1:T(8,128)S(1)}, u32[]{:S(2)}, u32[]{:S(2)}) collective-permute-start(f32[14,3,128]{2,0,1:T(8,128)S(1)} %get-tuple-element.128), channel_id=1, source_target_pairs={{1,0},{2,1},{3,2},{4,3},{5,4},{6,5},{7,6},{8,7},{9,8},{10,9},{11,1... | collective-permute-start | bytes 64520 | tf_op jit(solution)/shard_map/ppermute | solution.py:22
  39.3 2.3 %copy-start.2 = (f32[32,64]{0,1:T(8,128)}, f32[32,64]{0,1:T(8,128)S(1)}, u32[]{:S(2)}) copy-start(f32[32,64]{0,1:T(8,128)S(1)} %copy.40) | copy-start | bytes 24580
  53.5 3.1 %copy-start.3 = (f32[32,64]{0,1:T(8,128)S(1)}, f32[32,64]{0,1:T(8,128)}, u32[]{:S(2)}) copy-start(f32[32,64]{0,1:T(8,128)} %copy-done.2) | copy-start | bytes 24580
  70.2 6.8 %copy-start.4 = (f32[32,64]{0,1:T(8,128)S(1)}, f32[32,64]{0,1:T(8,128)}, u32[]{:S(2)}) copy-start(f32[32,64]{0,1:T(8,128)} %copy-done.2) | copy-start | bytes 24580
  77.0 6.0 %copy-start = (f32[4,8,8,128]{3,1,2,0:T(8,128)S(1)}, f32[4,8,8,128]{3,1,2,0:T(8,128)}, u32[]{:S(2)}) copy-start(f32[4,8,8,128]{3,1,2,0:T(8,128)} %copy.53) | copy-start | bytes 393220
  104.9 1.8 %collective-permute-start.4 = (f32[3,3,8,128]{3,2,1,0:T(8,128)S(1)}, f32[3,3,8,128]{3,2,1,0:T(8,128)S(1)}, u32[]{:S(2)}, u32[]{:S(2)}) collective-permute-start(f32[3,3,8,128]{3,2,1,0:T(8,128)S(1)} %get-tuple-element.122), channel_id=1, source_target_pairs={{0,480},{32,0},{64,32},{96,64},{128,96},{160,128},{192,160},{224,1... | collective-permute-start | bytes 110600 | tf_op jit(solution)/shard_map/ppermute | solution.py:30
  106.7 16.0 %collective-permute-start.5 = (f32[3,3,8,128]{3,2,1,0:T(8,128)S(1)}, f32[3,3,8,128]{3,2,1,0:T(8,128)S(1)}, u32[]{:S(2)}, u32[]{:S(2)}) collective-permute-start(f32[3,3,8,128]{3,2,1,0:T(8,128)S(1)} %collective-permute-done.4), channel_id=1, source_target_pairs={{0,31},{1,0},{2,1},{3,2},{4,3},{5,4},{6,5},{7,6},{8,7},{9,8},{10,9... | collective-permute-start | bytes 110600 | tf_op jit(solution)/shard_map/ppermute | solution.py:30
  114.1 8.7 %collective-permute-start.6 = (f32[3,4,8,128]{3,2,1,0:T(8,128)S(1)}, f32[3,4,8,128]{3,2,1,0:T(8,128)S(1)}, u32[]{:S(2)}, u32[]{:S(2)}) collective-permute-start(f32[3,4,8,128]{3,2,1,0:T(8,128)S(1)} %get-tuple-element.124), channel_id=1, source_target_pairs={{0,480},{32,0},{64,32},{96,64},{128,96},{160,128},{192,160},{224,1... | collective-permute-start | bytes 147464 | tf_op jit(solution)/shard_map/ppermute | solution.py:30
  116.8 5.9 %collective-permute-start.7 = (f32[3,3,8,128]{3,2,1,0:T(8,128)S(1)}, f32[3,3,8,128]{3,2,1,0:T(8,128)S(1)}, u32[]{:S(2)}, u32[]{:S(2)}) collective-permute-start(f32[3,3,8,128]{3,2,1,0:T(8,128)S(1)} %get-tuple-element.121), channel_id=1, source_target_pairs={{0,480},{32,0},{64,32},{96,64},{128,96},{160,128},{192,160},{224,1... | collective-permute-start | bytes 110600 | tf_op jit(solution)/shard_map/ppermute | solution.py:30
  116.9 18.3 %collective-permute-start.9 = (f32[8,3,8,128]{3,2,1,0:T(8,128)S(1)}, f32[8,3,8,128]{3,2,1,0:T(8,128)S(1)}, u32[]{:S(2)}, u32[]{:S(2)}) collective-permute-start(f32[8,3,8,128]{3,2,1,0:T(8,128)S(1)} %get-tuple-element.126), channel_id=1, source_target_pairs={{0,31},{1,0},{2,1},{3,2},{4,3},{5,4},{6,5},{7,6},{8,7},{9,8},{10,9... | collective-permute-start | bytes 294920 | tf_op jit(solution)/shard_map/ppermute | solution.py:30
  119.1 16.2 %collective-permute-start.10 = (f32[8,3,8,128]{3,2,1,0:T(8,128)S(1)}, f32[8,3,8,128]{3,2,1,0:T(8,128)S(1)}, u32[]{:S(2)}, u32[]{:S(2)}) collective-permute-start(f32[8,3,8,128]{3,2,1,0:T(8,128)S(1)} %get-tuple-element.125), channel_id=1, source_target_pairs={{0,1},{1,2},{2,3},{3,4},{4,5},{5,6},{6,7},{7,8},{8,9},{9,10},{10,1... | collective-permute-start | bytes 294920 | tf_op jit(solution)/shard_map/ppermute | solution.py:30
  122.7 4.6 %collective-permute-start.11 = (f32[3,3,8,128]{3,2,1,0:T(8,128)S(1)}, f32[3,3,8,128]{3,2,1,0:T(8,128)S(1)}, u32[]{:S(2)}, u32[]{:S(2)}) collective-permute-start(f32[3,3,8,128]{3,2,1,0:T(8,128)S(1)} %get-tuple-element.120), channel_id=1, source_target_pairs={{0,32},{32,64},{64,96},{96,128},{128,160},{160,192},{192,224},{224... | collective-permute-start | bytes 110600 | tf_op jit(solution)/shard_map/ppermute | solution.py:30
  122.8 4.9 %collective-permute-start.14 = (f32[3,3,8,128]{3,2,1,0:T(8,128)S(1)}, f32[3,3,8,128]{3,2,1,0:T(8,128)S(1)}, u32[]{:S(2)}, u32[]{:S(2)}) collective-permute-start(f32[3,3,8,128]{3,2,1,0:T(8,128)S(1)} %get-tuple-element.119), channel_id=1, source_target_pairs={{0,32},{32,64},{64,96},{96,128},{128,160},{160,192},{192,224},{224... | collective-permute-start | bytes 110600 | tf_op jit(solution)/shard_map/ppermute | solution.py:30
  122.8 10.4 %collective-permute-start.8 = (f32[3,3,8,128]{3,2,1,0:T(8,128)S(1)}, f32[3,3,8,128]{3,2,1,0:T(8,128)S(1)}, u32[]{:S(2)}, u32[]{:S(2)}) collective-permute-start(f32[3,3,8,128]{3,2,1,0:T(8,128)S(1)} %collective-permute-done.7), channel_id=1, source_target_pairs={{0,1},{1,2},{2,3},{3,4},{4,5},{5,6},{6,7},{7,8},{8,9},{9,10},{10,1... | collective-permute-start | bytes 110600 | tf_op jit(solution)/shard_map/ppermute | solution.py:30
  127.3 9.2 %collective-permute-start.13 = (f32[3,4,8,128]{3,2,1,0:T(8,128)S(1)}, f32[3,4,8,128]{3,2,1,0:T(8,128)S(1)}, u32[]{:S(2)}, u32[]{:S(2)}) collective-permute-start(f32[3,4,8,128]{3,2,1,0:T(8,128)S(1)} %get-tuple-element.123), channel_id=1, source_target_pairs={{0,32},{32,64},{64,96},{96,128},{128,160},{160,192},{192,224},{224... | collective-permute-start | bytes 147464 | tf_op jit(solution)/shard_map/ppermute | solution.py:30
  127.7 7.6 %collective-permute-start.12 = (f32[3,3,8,128]{3,2,1,0:T(8,128)S(1)}, f32[3,3,8,128]{3,2,1,0:T(8,128)S(1)}, u32[]{:S(2)}, u32[]{:S(2)}) collective-permute-start(f32[3,3,8,128]{3,2,1,0:T(8,128)S(1)} %collective-permute-done.11), channel_id=1, source_target_pairs={{0,31},{1,0},{2,1},{3,2},{4,3},{5,4},{6,5},{7,6},{8,7},{9,8},{10,9... | collective-permute-start | bytes 110600 | tf_op jit(solution)/shard_map/ppermute | solution.py:30
  133.3 9.2 %collective-permute-start.15 = (f32[3,3,8,128]{3,2,1,0:T(8,128)S(1)}, f32[3,3,8,128]{3,2,1,0:T(8,128)S(1)}, u32[]{:S(2)}, u32[]{:S(2)}) collective-permute-start(f32[3,3,8,128]{3,2,1,0:T(8,128)S(1)} %collective-permute-done.14), channel_id=1, source_target_pairs={{0,1},{1,2},{2,3},{3,4},{4,5},{5,6},{6,7},{7,8},{8,9},{9,10},{10,1... | collective-permute-start | bytes 110600 | tf_op jit(solution)/shard_map/ppermute | solution.py:30
  136.6 5.9 %copy-start.1 = (f32[8,4,8,128]{3,2,1,0:T(8,128)}, f32[8,4,8,128]{3,2,1,0:T(8,128)S(1)}, u32[]{:S(2)}) copy-start(f32[8,4,8,128]{3,2,1,0:T(8,128)S(1)} %get-tuple-element.113) | copy-start | bytes 393220
where the time goes:
time: 144 us; the launch traced here: 143 us
  starting transfers between devices  43.3 us (30%)
  other arithmetic  37.7 us (26%)
  local copies, waits for them, and re-layouts  31.6 us (22%)
  matrix products  19.7 us (14%)
  waiting for transfers between devices  10.3 us (7%)
    ppermute x12, starting transfers between devices, passed_along(): return lax.ppermute(value, axis, pairs)  25.7 us
    dot_general x3, matrix products, operate(): jnp.dot(scaled, stiffness, precision=lax.Precision.HIGHEST, preferred_ele...  19.7 us
    scatter-add x1, other arithmetic, per_device(): jnp.zeros((ext_rows * ext_cols, columns, dof_count), jnp.float32)  18.2 us
    ppermute x2, starting transfers between devices, padded(): lax.ppermute(lax.slice_in_dim(block, 0, width, axis=dim), axis, backward)  14.3 us
    reshape x3, local copies, waits for them, and re-layouts, correct(): spread = jnp.repeat(multiplier, group_size, axis=-1)  10.5 us
    ppermute x12, waiting for transfers between devices, passed_along(): return lax.ppermute(value, axis, pairs)  10.3 us
    reduce_sum x3, other arithmetic, correct(): weighted.reshape(patches, columns, groups, group_size).sum(-1)  9.39 us
    mul x3, local copies, waits for them, and re-layouts, correct(): weighted = residual * inverse[:, None, :]  9.05 us
  transfers between devices with their start and end apart: 16, of which 4 were waited for; matrix products, arithmetic and copies ran while one was open for 5% of the time, Pallas kernels for 0%

commit v1 on v0

v1 whole, which is shorter than its diff:
```python
import functools

import jax
import jax.numpy as jnp
from jax import lax
from jax.experimental import pallas as pl
from jax.experimental.pallas import tpu as pltpu
from jax.sharding import PartitionSpec as P

SLOTS = 8
NGRP = 8
REACH = 3
NCLASS = 4
ITERS = 3
BF16 = jnp.bfloat16
F32 = jnp.float32


def moved(value, axis, steps):
    count = lax.axis_size(axis)
    pairs = [(source, (source + steps) % count) for source in range(count)]
    return lax.ppermute(value, axis, pairs)


def swapped(value, axis, first):
    count = lax.axis_size(axis)
    pairs = [(k, (((k - first) ^ 1) + first) % count) for k in range(count)]
    return lax.ppermute(value, axis, pairs)


def scale_of(classes, contrast_ref):
    value = jnp.full(classes.shape, contrast_ref[0], F32)
    for k in range(1, NCLASS):
        value = jnp.where(classes == k, contrast_ref[k], value)
    return jnp.sqrt(value)


def split(value):
    high = value.astype(BF16)
    return high, (value - high.astype(F32)).astype(BF16)


def product(left, right):
    return jnp.dot(left, right, preferred_element_type=F32)


def group_ones(width, group):
    row = lax.broadcasted_iota(jnp.int32, (width, width), 0) // group
    col = lax.broadcasted_iota(jnp.int32, (width, width), 1) // group
    return jnp.where(row == col, 1.0, 0.0).astype(BF16)


def index_of(shift_x, shift_y, extent, places):
    _, col_count, row_count = shift_x.shape
    index_x = lax.broadcasted_iota(jnp.int32, shift_x.shape, 2) + shift_x
    index_y = lax.broadcasted_iota(jnp.int32, shift_y.shape, 1) + shift_y + col_count
    block = (index_y >= col_count).astype(jnp.int32) + (index_y >= 2 * col_count)
    col = index_y - block * col_count
    index = jnp.where(
        index_x < 0,
        places[3] + (block * REACH + index_x + REACH) * col_count + col,
        jnp.where(
            index_x >= row_count,
            places[4] + (block * REACH + index_x - row_count) * col_count + col,
            (block * row_count + index_x) * col_count + col,
        ),
    )
    slot = lax.broadcasted_iota(jnp.int32, shift_x.shape, 0) + 1
    return jnp.where(slot < extent, index, places[5])


def sides(near_ref, far_ref):
    even = lax.axis_index("yz") % 2 == 0
    near, far = near_ref[...], far_ref[...]
    return jnp.where(even, far, near), jnp.where(even, near, far)


def split_kernel(stiffness_ref, high_ref, low_ref):
    part = 64

    def step(k, carry):
        lines = pl.ds(pl.multiple_of(k * part, part), part)
        high_ref[lines, :], low_ref[lines, :] = split(stiffness_ref[lines, :])
        return carry

    lax.fori_loop(0, stiffness_ref.shape[0] // part, step, 0)


def pack_kernel(near_ref, far_ref, own_ref, last_out, first_out):
    left, right = sides(near_ref, far_ref)
    for k, block in enumerate((left, own_ref[...], right)):
        lines = slice(k * REACH, (k + 1) * REACH)
        last_out[lines] = block[block.shape[0] - REACH:]
        first_out[lines] = block[:REACH]


def solve_kernel(
    index_ref, contrast_ref, near_ref, own_ref, far_ref, above_ref, below_ref, coarse_ref,
    high_ref, low_ref,
    own_out, left_out, right_out, above_out, below_out,
    rows, spread, value, high, low, picture, weighted_high, weighted_low, total,
    *, row_count, col_count, dof, places,
):
    slots = SLOTS
    patches = row_count * col_count
    columns = coarse_ref.shape[0]
    own_place, empty = places[1], places[5]
    ones = group_ones(2 * dof, dof // NGRP)
    small = ones[:dof, :dof]
    rows[...] = jnp.full(rows.shape, 1.0, F32)
    left, right = sides(near_ref, far_ref)
    own_scale = scale_of(own_ref[...], contrast_ref)
    rows[pl.ds(places[0], patches), :] = scale_of(left, contrast_ref)
    rows[pl.ds(places[1], patches), :] = own_scale
    rows[pl.ds(places[2], patches), :] = scale_of(right, contrast_ref)
    for place, block in zip(places[3:], (above_ref, below_ref)):
        for x in range(block.shape[0]):
            rows[pl.ds(place + x * col_count, col_count), :] = scale_of(block[x], contrast_ref)
    inverse = 1.0 / rows[...]
    first, second = split(inverse * inverse)
    weight = product(first, small) + product(second, small)
    rows[...] = inverse * lax.rsqrt(weight)
    rows[pl.ds(empty, 8), :] = jnp.zeros((8, dof), F32)
    start = (own_scale[:, None, :] * coarse_ref[...][None]).reshape(patches * columns, dof)
    start_high, start_low = split(start)

    def tile(p, k):
        return slice(p * columns, (p + 1) * columns), slice(k * dof, (k + 1) * dof)

    def place_of(p, k):
        return index_ref[k - 1, p % col_count, p // col_count]

    for p in range(patches):
        for k in range(slots):
            row = rows[pl.ds(own_place + p if k == 0 else place_of(p, k), 1), :]
            spread[tile(p, k)] = jnp.broadcast_to(row, (columns, dof))

    pair = 2 * dof
    wide = 4 * dof
    for iteration in range(ITERS):
        for chunk in range(slots * dof // wide):
            lanes = slice(chunk * wide, (chunk + 1) * wide)
            if iteration == 0:
                image = (
                    product(start_high, high_ref[:dof, lanes])
                    + product(start_high, low_ref[:dof, lanes])
                    + product(start_low, high_ref[:dof, lanes])
                )
            else:
                source = (iteration - 1) % 2
                image = (
                    product(high[source], high_ref[:, lanes])
                    + product(high[source], low_ref[:, lanes])
                    + product(low[source], high_ref[:, lanes])
                )
            picture[:, lanes] = image
            first, second = split(spread[:, lanes] * image)
            weighted_high[:, lanes] = first
            weighted_low[:, lanes] = second
        for chunk in range(slots * dof // pair):
            lanes = slice(chunk * pair, (chunk + 1) * pair)
            factor = spread[:, lanes]
            mean = product(weighted_high[:, lanes], ones) + product(weighted_low[:, lanes], ones)
            change = jnp.where(factor > 0.0, picture[:, lanes] - factor * mean, 0.0)
            result = -change if iteration == 0 else value[:, lanes] - change
            value[:, lanes] = result
            if iteration < ITERS - 1:
                if chunk == 0:
                    result = jnp.concatenate(
                        [result[:, :dof] + start, result[:, dof:]], axis=1
                    )
                first, second = split(result)
                high[iteration % 2, :, lanes] = first
                low[iteration % 2, :, lanes] = second

    total[...] = jnp.zeros(total.shape, F32)
    for p in range(patches):
        total[own_place + p] = value[tile(p, 0)]
    for p in range(patches):
        spots = [place_of(p, k) for k in range(1, slots)]
        sums = [total[spots[k - 1]] + value[tile(p, k)] for k in range(1, slots)]
        for spot, entry in zip(spots, sums):
            total[spot] = entry
    own_out[...] = total[pl.ds(own_place, patches)].reshape(own_out.shape)
    for x in range(row_count):
        for y in range(REACH):
            left_out[x, y] = total[places[0] + x * col_count + y + col_count - REACH]
            right_out[x, y] = total[places[2] + x * col_count + y]
    for place, out in ((places[3], above_out), (places[4], below_out)):
        for x in range(REACH):
            for y in range(col_count + 2 * REACH):
                block, col = divmod(y - REACH + col_count, col_count)
                out[x, y] = total[place + (block * REACH + x) * col_count + col]


def joined_kernel(left_ref, right_ref, from_below, from_above, near_out, far_out):
    row_count, reach = left_ref.shape[:2]
    last = from_below.shape[1] - reach

    def join(source, columns, out):
        out[...] = source[...]
        out[row_count - reach:] = out[row_count - reach:] + from_below[:, columns]
        out[:reach] = out[:reach] + from_above[:, columns]

    def both(left_out, right_out):
        join(left_ref, slice(0, reach), left_out)
        join(right_ref, slice(last, last + reach), right_out)

    even = lax.axis_index("yz") % 2 == 0
    pl.when(even)(lambda: both(far_out, near_out))
    pl.when(jnp.logical_not(even))(lambda: both(near_out, far_out))


def final_kernel(
    contrast_ref, classes_ref, own_ref, near_ref, far_ref, from_below, from_above, out
):
    row_count, count = own_ref.shape[:2]
    reach = near_ref.shape[1]
    from_left, from_right = sides(near_ref, far_ref)
    middle = slice(reach, reach + count)
    inverse = 1.0 / scale_of(classes_ref[...], contrast_ref)
    out[...] = own_ref[...]
    out[:, count - reach:] = out[:, count - reach:] + from_right
    out[:, :reach] = out[:, :reach] + from_left
    out[row_count - reach:] = out[row_count - reach:] + from_below[:, middle]
    out[:reach] = out[:reach] + from_above[:, middle]
    out[...] = out[...] * inverse[:, :, None, :]


SMEM = pl.BlockSpec(memory_space=pltpu.SMEM)
VMEM = pl.BlockSpec(memory_space=pltpu.VMEM)


def grant(mebibytes):
    return pltpu.CompilerParams(vmem_limit_bytes=mebibytes * 1024 * 1024)


def shapes(*dims):
    return jax.ShapeDtypeStruct(dims, F32)


def per_device(classes, contrast, shift_x, shift_y, extent, coarse_basis, stiffness):
    row_count, col_count, dof = classes.shape
    columns = coarse_basis.shape[0]
    order = SLOTS * dof
    patches = row_count * col_count
    edge = 3 * REACH * col_count
    places = [0, patches, 2 * patches, 3 * patches]
    places += [places[3] + (edge + 7) // 8 * 8]
    places += [places[4] + (edge + 7) // 8 * 8]
    empty = places[5]

    far = swapped(classes, "yz", 1)
    near = swapped(classes, "yz", 0)

    index = index_of(
        shift_x.transpose(2, 1, 0), shift_y.transpose(2, 1, 0), extent.T, places
    )
    stiff = jax.ShapeDtypeStruct((order, order), BF16)
    stiff_high, stiff_low = pl.pallas_call(
        split_kernel,
        in_specs=[VMEM],
        out_specs=[VMEM] * 2,
        out_shape=[stiff, stiff],
        compiler_params=grant(4),
        cost_estimate=pl.CostEstimate(
            flops=2 * order * order, bytes_accessed=8 * order * order, transcendentals=0
        ),
        name="split",
    )(stiffness)
    near, far, stiff_high, stiff_low, index = lax.optimization_barrier(
        (near, far, stiff_high, stiff_low, index)
    )
    halo = jax.ShapeDtypeStruct((3 * REACH, col_count, dof), jnp.int32)
    last_rows, first_rows = pl.pallas_call(
        pack_kernel,
        in_specs=[VMEM] * 3,
        out_specs=[VMEM] * 2,
        out_shape=[halo, halo],
        compiler_params=grant(4),
        name="pack",
    )(near, far, classes)
    above = moved(last_rows, "gx", 1)
    below = moved(first_rows, "gx", -1)

    ext_cols = col_count + 2 * REACH
    whole = (row_count, col_count, columns, dof)
    own_sum, left_sum, right_sum, above_sum, below_sum = pl.pallas_call(
        functools.partial(
            solve_kernel, row_count=row_count, col_count=col_count, dof=dof, places=places
        ),
        in_specs=[SMEM, SMEM] + [VMEM] * 8,
        out_specs=[VMEM] * 5,
        out_shape=[
            shapes(*whole),
            shapes(row_count, REACH, columns, dof),
            shapes(row_count, REACH, columns, dof),
            shapes(REACH, ext_cols, columns, dof),
            shapes(REACH, ext_cols, columns, dof),
        ],
        scratch_shapes=[
            pltpu.VMEM((empty + 8, dof), F32),
            pltpu.VMEM((patches * columns, order), F32),
            pltpu.VMEM((patches * columns, order), F32),
            pltpu.VMEM((2, patches * columns, order), BF16),
            pltpu.VMEM((2, patches * columns, order), BF16),
            pltpu.VMEM((patches * columns, order), F32),
            pltpu.VMEM((patches * columns, order), BF16),
            pltpu.VMEM((patches * columns, order), BF16),
            pltpu.VMEM((empty + 1, columns, dof), F32),
        ],
        compiler_params=grant(14),
        name="solve",
    )(
        index, contrast, near.reshape(patches, dof), classes.reshape(patches, dof),
        far.reshape(patches, dof), above, below, coarse_basis, stiff_high, stiff_low,
    )

    from_below = moved(above_sum, "gx", -1)
    from_above = moved(below_sum, "gx", 1)
    side = shapes(row_count, REACH, columns, dof)
    near_sum, far_sum = pl.pallas_call(
        joined_kernel,
        in_specs=[VMEM] * 4,
        out_specs=[VMEM] * 2,
        out_shape=[side, side],
        compiler_params=grant(4),
        name="joined",
    )(left_sum, right_sum, from_below, from_above)
    far_sum = swapped(far_sum, "yz", 1)
    near_sum = swapped(near_sum, "yz", 0)
    return pl.pallas_call(
        final_kernel,
        in_specs=[SMEM] + [VMEM] * 6,
        out_specs=VMEM,
        out_shape=shapes(*whole),
        compiler_params=grant(4),
        name="final",
    )(contrast, classes, own_sum, near_sum, far_sum, from_below, from_above)


def solution(mesh):
    return jax.shard_map(
        per_device,
        mesh=mesh,
        in_specs=(
            P("gx", "yz", None),
            P(),
            P("gx", "yz", None),
            P("gx", "yz", None),
            P("gx", "yz"),
            P(),
            P(),
        ),
        out_specs=P("gx", "yz", None, None),
        check_vma=False,
    )
```

time: 144 us -> 49.9 us (0.35)
  the two profiles are of different devices: /device:TPU:32 before, /device:TPU:30 now
where the time goes in v1:
time: 49.9 us; the launch traced here: 49.6 us
  starting transfers between devices  25.8 us (52%)
  waiting for transfers between devices  12.4 us (25%)
  Pallas kernels  8.27 us (17%)
  local copies, waits for them, and re-layouts  2.19 us (4%)
  other arithmetic  0.81 us (2%)
    ppermute x4, starting transfers between devices, swapped(): return lax.ppermute(value, axis, pairs)  14.7 us
    ppermute x4, starting transfers between devices, moved(): return lax.ppermute(value, axis, pairs)  11 us
    ppermute x4, waiting for transfers between devices, moved(): return lax.ppermute(value, axis, pairs)  6.97 us
    pallas_call x1, Pallas kernels, per_device(): pl.pallas_call(functools.partial(solve_kernel, row_count=row_count, col_c...  6.28 us
    ppermute x4, waiting for transfers between devices, swapped(): return lax.ppermute(value, axis, pairs)  5.44 us
    unnamed x8, local copies, waits for them, and re-layouts  2.19 us
    pallas_call x1, Pallas kernels, per_device(): pl.pallas_call(final_kernel, in_specs=[SMEM] + [VMEM] * 6, out_specs=VMEM...  1.26 us
  transfers between devices with their start and end apart: 8, of which 5 were waited for; matrix products, arithmetic and copies ran while one was open for 2% of the time, Pallas kernels for 1%

profile of v1, /device:TPU:30, one launch (start us, length us, event | category | flops | bytes accessed | tf_op | source)
XLA Modules:
  0.0 49.6 jit_solution(3469917201933392824)
XLA Ops:
  0.0 4.6 %collective-permute-start.1 = (s32[8,4,128]{2,1,0:T(4,128)}, s32[8,4,128]{2,1,0:T(4,128)S(1)}, u32[]{:S(2)}, u32[]{:S(2)}) collective-permute-start(s32[8,4,128]{2,1,0:T(4,128)} %classes_ref.1), channel_id=1, source_target_pairs={{0,31},{1,2},{2,1},{3,4},{4,3},{5,6},{6,5},{7,8},{8,7},{9,10},{10,... | collective-permute-start | bytes 49160 | tf_op jit(solution)/shard_map/ppermute | solution.py:28
  4.6 1.9 %collective-permute-start = (s32[8,4,128]{2,1,0:T(4,128)}, s32[8,4,128]{2,1,0:T(4,128)S(1)}, u32[]{:S(2)}, u32[]{:S(2)}) collective-permute-start(s32[8,4,128]{2,1,0:T(4,128)} %classes_ref.1), channel_id=1, source_target_pairs={{0,1},{1,0},{2,3},{3,2},{4,5},{5,4},{6,7},{7,6},{8,9},{9,8},{10,11... | collective-permute-start | bytes 49160 | tf_op jit(solution)/shard_map/ppermute | solution.py:28
  6.5 0.8 %select_select_fusion.index_ref = s32[7,4,8]{2,1,0:T(4,128)S(1)} fusion(s32[8,4,7]{0,1,2:T(4,128)} %param.10, s32[8,4,7]{0,1,2:T(4,128)} %param.9, s32[4,8]{1,0:T(4,128)} %bitcast.17, s32[7]{0:T(128)S(1)} %iota_add_fusion), kind=kLoop, calls=%fused_computation.3 | loop fusion | flops 6720 | bytes 2844 | tf_op jit(solution)/shard_map/jit(_where)/select_n | solution.py:69
  7.4 2.2 %copy-done = f32[1024,1024]{1,0:T(8,128)S(1)} copy-done((f32[1024,1024]{1,0:T(8,128)S(1)}, f32[1024,1024]{1,0:T(8,128)}, u32[]{:S(2)}) %copy-start) | copy-done | bytes 4194328
  9.6 0.7 %split.1 = (bf16[1024,1024]{1,0:T(8,128)(2,1)S(1)}, bf16[1024,1024]{1,0:T(8,128)(2,1)S(1)}) custom-call(f32[1024,1024]{1,0:T(8,128)S(1)} %copy-done), custom_call_target="tpu_custom_call" | custom-call | flops 2097152 | bytes 8388608 | tf_op jit(solution)/shard_map/split/pallas_call | solution.py:260
  10.3 0.0 collective-permute-done.1.far_ref
  10.3 0.2 collective-permute-done.near_ref
  10.5 0.0 copy-done.1
  10.5 0.0 collective-permute-start.2
  10.5 8.1 %collective-permute-start.3 = (s32[9,4,128]{2,1,0:T(4,128)S(1)}, s32[9,4,128]{2,1,0:T(4,128)S(1)}, u32[]{:S(2)}, u32[]{:S(2)}) collective-permute-start(s32[9,4,128]{2,1,0:T(4,128)S(1)} %get-tuple-element.27), channel_id=1, source_target_pairs={{0,480},{32,0},{64,32},{96,64},{128,96},{160,128},{192,160},{224,1... | collective-permute-start | bytes 55304 | tf_op jit(solution)/shard_map/ppermute | solution.py:22
  18.6 1.4 %collective-permute-done.2.above_ref = s32[9,4,128]{2,1,0:T(4,128)S(1)} collective-permute-done((s32[9,4,128]{2,1,0:T(4,128)S(1)}, s32[9,4,128]{2,1,0:T(4,128)S(1)}, u32[]{:S(2)}, u32[]{:S(2)}) %collective-permute-start.2) | collective-permute-done | bytes 18464 | tf_op jit(solution)/shard_map/ppermute | solution.py:22
  20.0 0.0 collective-permute-done.3.below_ref
  20.0 0.0 copy-done.2
  20.0 0.0 copy-done.3
  20.0 6.3 %solve.1 = (f32[8,4,8,128]{3,2,1,0:T(8,128)S(1)}, f32[8,3,8,128]{3,2,1,0:T(8,128)S(1)}, f32[8,3,8,128]{3,2,1,0:T(8,128)S(1)}, f32[3,10,8,128]{3,2,1,0:T(8,128)S(1)}, f32[3,10,8,128]{3,2,1,0:T(8,128)S(1)}) custom-call(s32[7,4,8]{2,1,0:T(4,128)S(1)} %select_select_fusion.index_ref, f32[4]{0:T(128)S(1)} %copy-done.3, s32[32,128]{1,0:T(8,128)S(1)} %bitcast.16, ...), custom_call_target="tpu_custom_call" | custom-call | tf_op jit(solution)/shard_map/solve/pallas_call | solution.py:288
  26.3 2.9 %collective-permute-start.4 = (f32[3,10,8,128]{3,2,1,0:T(8,128)S(1)}, f32[3,10,8,128]{3,2,1,0:T(8,128)S(1)}, u32[]{:S(2)}, u32[]{:S(2)}) collective-permute-start(f32[3,10,8,128]{3,2,1,0:T(8,128)S(1)} %get-tuple-element.33), channel_id=1, source_target_pairs={{0,480},{32,0},{64,32},{96,64},{128,96},{160,128},{192,160},{224,1... | collective-permute-start | bytes 368648 | tf_op jit(solution)/shard_map/ppermute | solution.py:22
  29.3 0.0 collective-permute-start.5
  29.3 2.4 %collective-permute-done.4.from_below = f32[3,10,8,128]{3,2,1,0:T(8,128)S(1)} collective-permute-done((f32[3,10,8,128]{3,2,1,0:T(8,128)S(1)}, f32[3,10,8,128]{3,2,1,0:T(8,128)S(1)}, u32[]{:S(2)}, u32[]{:S(2)}) %collective-permute-start.4) | collective-permute-done | bytes 122912 | tf_op jit(solution)/shard_map/ppermute | solution.py:22
  31.7 3.1 %collective-permute-done.5.from_above = f32[3,10,8,128]{3,2,1,0:T(8,128)S(1)} collective-permute-done((f32[3,10,8,128]{3,2,1,0:T(8,128)S(1)}, f32[3,10,8,128]{3,2,1,0:T(8,128)S(1)}, u32[]{:S(2)}, u32[]{:S(2)}) %collective-permute-start.5) | collective-permute-done | bytes 122912 | tf_op jit(solution)/shard_map/ppermute | solution.py:22
  34.8 3.7 %collective-permute-start.6 = (f32[8,3,8,128]{3,2,1,0:T(8,128)S(1)}, f32[8,3,8,128]{3,2,1,0:T(8,128)S(1)}, u32[]{:S(2)}, u32[]{:S(2)}) collective-permute-start(f32[8,3,8,128]{3,2,1,0:T(8,128)S(1)} %get-tuple-element.35), channel_id=1, source_target_pairs={{0,1},{1,0},{2,3},{3,2},{4,5},{5,4},{6,7},{7,6},{8,9},{9,8},{10,11... | collective-permute-start | bytes 294920 | tf_op jit(solution)/shard_map/ppermute | solution.py:28
  38.5 4.6 %collective-permute-start.7 = (f32[8,3,8,128]{3,2,1,0:T(8,128)S(1)}, f32[8,3,8,128]{3,2,1,0:T(8,128)S(1)}, u32[]{:S(2)}, u32[]{:S(2)}) collective-permute-start(f32[8,3,8,128]{3,2,1,0:T(8,128)S(1)} %get-tuple-element.36), channel_id=1, source_target_pairs={{0,31},{1,2},{2,1},{3,4},{4,3},{5,6},{6,5},{7,8},{8,7},{9,10},{10,... | collective-permute-start | bytes 294920 | tf_op jit(solution)/shard_map/ppermute | solution.py:28
  43.0 0.0 collective-permute-done.6.near_ref
  43.0 5.3 %collective-permute-done.7.far_ref = f32[8,3,8,128]{3,2,1,0:T(8,128)S(1)} collective-permute-done((f32[8,3,8,128]{3,2,1,0:T(8,128)S(1)}, f32[8,3,8,128]{3,2,1,0:T(8,128)S(1)}, u32[]{:S(2)}, u32[]{:S(2)}) %collective-permute-start.7) | collective-permute-done | bytes 98336 | tf_op jit(solution)/shard_map/ppermute | solution.py:28
  48.3 1.3 %final.1 = f32[8,4,8,128]{3,2,1,0:T(8,128)} custom-call(f32[4]{0:T(128)S(1)} %copy-done.3, s32[8,4,128]{2,1,0:T(4,128)S(1)} %copy-done.1, f32[8,4,8,128]{3,2,1,0:T(8,128)S(1)} %get-tuple-element.30.own_ref, f32[8,3,8,128]{3,2,1,0:T(8,128)S(1)} %collective-permute-done.6.near_ref, f32[8,3,8,128]{3,2,1,0:T(8,128)S(1)} %collective-permute-done.7.far_ref, ...), custom_call_target="tpu_custom_call" | custom-call | tf_op jit(solution)/shard_map/final/pallas_call | solution.py:332
  (7 shorter events, 0.0 us)
Async XLA Ops:
  0.0 10.3 %collective-permute-start.1 = (s32[8,4,128]{2,1,0:T(4,128)}, s32[8,4,128]{2,1,0:T(4,128)S(1)}, u32[]{:S(2)}, u32[]{:S(2)}) collective-permute-start(s32[8,4,128]{2,1,0:T(4,128)} %classes_ref.1), channel_id=1, source_target_pairs={{0,31},{1,2},{2,1},{3,4},{4,3},{5,6},{6,5},{7,8},{8,7},{9,10},{10,... | collective-permute-start | bytes 49160 | tf_op jit(solution)/shard_map/ppermute | solution.py:28
  4.6 5.8 %collective-permute-start = (s32[8,4,128]{2,1,0:T(4,128)}, s32[8,4,128]{2,1,0:T(4,128)S(1)}, u32[]{:S(2)}, u32[]{:S(2)}) collective-permute-start(s32[8,4,128]{2,1,0:T(4,128)} %classes_ref.1), channel_id=1, source_target_pairs={{0,1},{1,0},{2,3},{3,2},{4,5},{5,4},{6,7},{7,6},{8,9},{9,8},{10,11... | collective-permute-start | bytes 49160 | tf_op jit(solution)/shard_map/ppermute | solution.py:28
  7.4 2.2 %copy-start = (f32[1024,1024]{1,0:T(8,128)S(1)}, f32[1024,1024]{1,0:T(8,128)}, u32[]{:S(2)}) copy-start(f32[1024,1024]{1,0:T(8,128)} %stiffness_ref.1) | copy-start | bytes 12582916
  9.5 0.9 %copy-start.1 = (s32[8,4,128]{2,1,0:T(4,128)S(1)}, s32[8,4,128]{2,1,0:T(4,128)}, u32[]{:S(2)}) copy-start(s32[8,4,128]{2,1,0:T(4,128)} %classes_ref.1) | copy-start | bytes 49156
  9.6 10.5 %copy-start.2 = (f32[8,128]{1,0:T(8,128)S(1)}, f32[8,128]{1,0:T(8,128)}, u32[]{:S(2)}) copy-start(f32[8,128]{1,0:T(8,128)} %coarse_ref.1) | copy-start | bytes 12292
  9.6 10.5 %copy-start.3 = (f32[4]{0:T(128)S(1)}, f32[4]{0:T(128)}, u32[]{:S(2)}) copy-start(f32[4]{0:T(128)} %contrast_ref.3) | copy-start | bytes 52
  10.5 9.5 %collective-permute-start.2 = (s32[9,4,128]{2,1,0:T(4,128)S(1)}, s32[9,4,128]{2,1,0:T(4,128)S(1)}, u32[]{:S(2)}, u32[]{:S(2)}) collective-permute-start(s32[9,4,128]{2,1,0:T(4,128)S(1)} %get-tuple-element.26), channel_id=1, source_target_pairs={{0,32},{32,64},{64,96},{96,128},{128,160},{160,192},{192,224},{224... | collective-permute-start | bytes 55304 | tf_op jit(solution)/shard_map/ppermute | solution.py:22
  10.5 9.5 %collective-permute-start.3 = (s32[9,4,128]{2,1,0:T(4,128)S(1)}, s32[9,4,128]{2,1,0:T(4,128)S(1)}, u32[]{:S(2)}, u32[]{:S(2)}) collective-permute-start(s32[9,4,128]{2,1,0:T(4,128)S(1)} %get-tuple-element.27), channel_id=1, source_target_pairs={{0,480},{32,0},{64,32},{96,64},{128,96},{160,128},{192,160},{224,1... | collective-permute-start | bytes 55304 | tf_op jit(solution)/shard_map/ppermute | solution.py:22
  26.3 5.4 %collective-permute-start.4 = (f32[3,10,8,128]{3,2,1,0:T(8,128)S(1)}, f32[3,10,8,128]{3,2,1,0:T(8,128)S(1)}, u32[]{:S(2)}, u32[]{:S(2)}) collective-permute-start(f32[3,10,8,128]{3,2,1,0:T(8,128)S(1)} %get-tuple-element.33), channel_id=1, source_target_pairs={{0,480},{32,0},{64,32},{96,64},{128,96},{160,128},{192,160},{224,1... | collective-permute-start | bytes 368648 | tf_op jit(solution)/shard_map/ppermute | solution.py:22
  29.3 5.5 %collective-permute-start.5 = (f32[3,10,8,128]{3,2,1,0:T(8,128)S(1)}, f32[3,10,8,128]{3,2,1,0:T(8,128)S(1)}, u32[]{:S(2)}, u32[]{:S(2)}) collective-permute-start(f32[3,10,8,128]{3,2,1,0:T(8,128)S(1)} %get-tuple-element.34), channel_id=1, source_target_pairs={{0,32},{32,64},{64,96},{96,128},{128,160},{160,192},{192,224},{224... | collective-permute-start | bytes 368648 | tf_op jit(solution)/shard_map/ppermute | solution.py:22
  34.8 8.2 %collective-permute-start.6 = (f32[8,3,8,128]{3,2,1,0:T(8,128)S(1)}, f32[8,3,8,128]{3,2,1,0:T(8,128)S(1)}, u32[]{:S(2)}, u32[]{:S(2)}) collective-permute-start(f32[8,3,8,128]{3,2,1,0:T(8,128)S(1)} %get-tuple-element.35), channel_id=1, source_target_pairs={{0,1},{1,0},{2,3},{3,2},{4,5},{5,4},{6,7},{7,6},{8,9},{9,8},{10,11... | collective-permute-start | bytes 294920 | tf_op jit(solution)/shard_map/ppermute | solution.py:28
  38.5 9.8 %collective-permute-start.7 = (f32[8,3,8,128]{3,2,1,0:T(8,128)S(1)}, f32[8,3,8,128]{3,2,1,0:T(8,128)S(1)}, u32[]{:S(2)}, u32[]{:S(2)}) collective-permute-start(f32[8,3,8,128]{3,2,1,0:T(8,128)S(1)} %get-tuple-element.36), channel_id=1, source_target_pairs={{0,31},{1,2},{2,1},{3,4},{4,3},{5,6},{6,5},{7,8},{8,7},{9,10},{10,... | collective-permute-start | bytes 294920 | tf_op jit(solution)/shard_map/ppermute | solution.py:28

commit v2 on v1

--- a/solution.py
+++ b/solution.py
@@ -97,7 +97,7 @@
 def solve_kernel(
     index_ref, contrast_ref, near_ref, own_ref, far_ref, above_ref, below_ref, coarse_ref,
     high_ref, low_ref,
-    own_out, left_out, right_out, above_out, below_out,
+    own_out, left_out, right_out, below_out, above_out,
     rows, spread, value, high, low, picture, weighted_high, weighted_low, total,
     *, row_count, col_count, dof, places,
 ):
@@ -193,7 +193,7 @@
                 out[x, y] = total[place + (block * REACH + x) * col_count + col]
 
 
-def joined_kernel(left_ref, right_ref, from_below, from_above, near_out, far_out):
+def joined_kernel(left_ref, right_ref, from_above, from_below, far_out, near_out):
     row_count, reach = left_ref.shape[:2]
     last = from_below.shape[1] - reach
 
@@ -212,7 +212,7 @@
 
 
 def final_kernel(
-    contrast_ref, classes_ref, own_ref, near_ref, far_ref, from_below, from_above, out
+    contrast_ref, classes_ref, own_ref, far_ref, near_ref, from_above, from_below, out
 ):
     row_count, count = own_ref.shape[:2]
     reach = near_ref.shape[1]
@@ -285,7 +285,7 @@
 
     ext_cols = col_count + 2 * REACH
     whole = (row_count, col_count, columns, dof)
-    own_sum, left_sum, right_sum, above_sum, below_sum = pl.pallas_call(
+    own_sum, left_sum, right_sum, below_sum, above_sum = pl.pallas_call(
         functools.partial(
             solve_kernel, row_count=row_count, col_count=col_count, dof=dof, places=places
         ),
@@ -319,14 +319,14 @@
     from_below = moved(above_sum, "gx", -1)
     from_above = moved(below_sum, "gx", 1)
     side = shapes(row_count, REACH, columns, dof)
-    near_sum, far_sum = pl.pallas_call(
+    far_sum, near_sum = pl.pallas_call(
         joined_kernel,
         in_specs=[VMEM] * 4,
         out_specs=[VMEM] * 2,
         out_shape=[side, side],
         compiler_params=grant(4),
         name="joined",
-    )(left_sum, right_sum, from_below, from_above)
+    )(left_sum, right_sum, from_above, from_below)
     far_sum = swapped(far_sum, "yz", 1)
     near_sum = swapped(near_sum, "yz", 0)
     return pl.pallas_call(
@@ -336,7 +336,7 @@
         out_shape=shapes(*whole),
         compiler_params=grant(4),
         name="final",
-    )(contrast, classes, own_sum, near_sum, far_sum, from_below, from_above)
+    )(contrast, classes, own_sum, far_sum, near_sum, from_above, from_below)
 
 
 def solution(mesh):

time: 49.9 us -> 45.7 us (0.916)
  the two profiles are of different devices: /device:TPU:30 before, /device:TPU:4 now
where the time goes in v2:
time: 45.7 us; the launch traced here: 45.3 us
  starting transfers between devices  25.3 us (55%)
  waiting for transfers between devices  8.6 us (19%)
  Pallas kernels  8.28 us (18%)
  local copies, waits for them, and re-layouts  2.19 us (5%)
  other arithmetic  0.81 us (2%)
    ppermute x4, starting transfers between devices, swapped(): return lax.ppermute(value, axis, pairs)  14.4 us
    ppermute x4, starting transfers between devices, moved(): return lax.ppermute(value, axis, pairs)  10.9 us
    pallas_call x1, Pallas kernels, per_device(): pl.pallas_call(functools.partial(solve_kernel, row_count=row_count, col_c...  6.28 us
    ppermute x4, waiting for transfers between devices, swapped(): return lax.ppermute(value, axis, pairs)  4.59 us
    ppermute x4, waiting for transfers between devices, moved(): return lax.ppermute(value, axis, pairs)  4.01 us
    unnamed x8, local copies, waits for them, and re-layouts  2.19 us
    pallas_call x1, Pallas kernels, per_device(): pl.pallas_call(final_kernel, in_specs=[SMEM] + [VMEM] * 6, out_specs=VMEM...  1.26 us
  transfers between devices with their start and end apart: 8, of which 4 were waited for; matrix products, arithmetic and copies ran while one was open for 2% of the time, Pallas kernels for 2%

profile of v2, /device:TPU:4, one launch (start us, length us, event | category | flops | bytes accessed | tf_op | source)
XLA Modules:
  0.0 45.3 jit_solution(9528290726067069173)
XLA Ops:
  0.0 2.4 %collective-permute-start.1 = (s32[8,4,128]{2,1,0:T(4,128)}, s32[8,4,128]{2,1,0:T(4,128)S(1)}, u32[]{:S(2)}, u32[]{:S(2)}) collective-permute-start(s32[8,4,128]{2,1,0:T(4,128)} %classes_ref.1), channel_id=1, source_target_pairs={{0,31},{1,2},{2,1},{3,4},{4,3},{5,6},{6,5},{7,8},{8,7},{9,10},{10,... | collective-permute-start | bytes 49160 | tf_op jit(solution)/shard_map/ppermute | solution.py:28
  2.4 4.1 %collective-permute-start = (s32[8,4,128]{2,1,0:T(4,128)}, s32[8,4,128]{2,1,0:T(4,128)S(1)}, u32[]{:S(2)}, u32[]{:S(2)}) collective-permute-start(s32[8,4,128]{2,1,0:T(4,128)} %classes_ref.1), channel_id=1, source_target_pairs={{0,1},{1,0},{2,3},{3,2},{4,5},{5,4},{6,7},{7,6},{8,9},{9,8},{10,11... | collective-permute-start | bytes 49160 | tf_op jit(solution)/shard_map/ppermute | solution.py:28
  6.5 0.8 %select_select_fusion.index_ref = s32[7,4,8]{2,1,0:T(4,128)S(1)} fusion(s32[8,4,7]{0,1,2:T(4,128)} %param.10, s32[8,4,7]{0,1,2:T(4,128)} %param.9, s32[4,8]{1,0:T(4,128)} %bitcast.17, s32[7]{0:T(128)S(1)} %iota_add_fusion), kind=kLoop, calls=%fused_computation.3 | loop fusion | flops 6720 | bytes 2844 | tf_op jit(solution)/shard_map/jit(_where)/select_n | solution.py:69
  7.3 2.2 %copy-done = f32[1024,1024]{1,0:T(8,128)S(1)} copy-done((f32[1024,1024]{1,0:T(8,128)S(1)}, f32[1024,1024]{1,0:T(8,128)}, u32[]{:S(2)}) %copy-start) | copy-done | bytes 4194328
  9.5 0.7 %split.1 = (bf16[1024,1024]{1,0:T(8,128)(2,1)S(1)}, bf16[1024,1024]{1,0:T(8,128)(2,1)S(1)}) custom-call(f32[1024,1024]{1,0:T(8,128)S(1)} %copy-done), custom_call_target="tpu_custom_call" | custom-call | flops 2097152 | bytes 8388608 | tf_op jit(solution)/shard_map/split/pallas_call | solution.py:260
  10.2 0.0 collective-permute-done.1.far_ref
  10.3 0.0 collective-permute-done.near_ref
  10.3 0.0 copy-done.1
  10.3 0.0 collective-permute-start.2
  10.3 7.9 %collective-permute-start.3 = (s32[9,4,128]{2,1,0:T(4,128)S(1)}, s32[9,4,128]{2,1,0:T(4,128)S(1)}, u32[]{:S(2)}, u32[]{:S(2)}) collective-permute-start(s32[9,4,128]{2,1,0:T(4,128)S(1)} %get-tuple-element.27), channel_id=1, source_target_pairs={{0,480},{32,0},{64,32},{96,64},{128,96},{160,128},{192,160},{224,1... | collective-permute-start | bytes 55304 | tf_op jit(solution)/shard_map/ppermute | solution.py:22
  18.3 1.4 %collective-permute-done.2.above_ref = s32[9,4,128]{2,1,0:T(4,128)S(1)} collective-permute-done((s32[9,4,128]{2,1,0:T(4,128)S(1)}, s32[9,4,128]{2,1,0:T(4,128)S(1)}, u32[]{:S(2)}, u32[]{:S(2)}) %collective-permute-start.2) | collective-permute-done | bytes 18464 | tf_op jit(solution)/shard_map/ppermute | solution.py:22
  19.7 0.0 collective-permute-done.3.below_ref
  19.7 0.0 copy-done.2
  19.7 0.0 copy-done.3
  19.7 6.3 %solve.1 = (f32[8,4,8,128]{3,2,1,0:T(8,128)S(1)}, f32[8,3,8,128]{3,2,1,0:T(8,128)S(1)}, f32[8,3,8,128]{3,2,1,0:T(8,128)S(1)}, f32[3,10,8,128]{3,2,1,0:T(8,128)S(1)}, f32[3,10,8,128]{3,2,1,0:T(8,128)S(1)}) custom-call(s32[7,4,8]{2,1,0:T(4,128)S(1)} %select_select_fusion.index_ref, f32[4]{0:T(128)S(1)} %copy-done.3, s32[32,128]{1,0:T(8,128)S(1)} %bitcast.16, ...), custom_call_target="tpu_custom_call" | custom-call | tf_op jit(solution)/shard_map/solve/pallas_call | solution.py:288
  26.0 0.0 collective-permute-start.4
  26.0 3.0 %collective-permute-start.5 = (f32[3,10,8,128]{3,2,1,0:T(8,128)S(1)}, f32[3,10,8,128]{3,2,1,0:T(8,128)S(1)}, u32[]{:S(2)}, u32[]{:S(2)}) collective-permute-start(f32[3,10,8,128]{3,2,1,0:T(8,128)S(1)} %get-tuple-element.34), channel_id=1, source_target_pairs={{0,480},{32,0},{64,32},{96,64},{128,96},{160,128},{192,160},{224,1... | collective-permute-start | bytes 368648 | tf_op jit(solution)/shard_map/ppermute | solution.py:22
  29.0 2.5 %collective-permute-done.4.from_above = f32[3,10,8,128]{3,2,1,0:T(8,128)S(1)} collective-permute-done((f32[3,10,8,128]{3,2,1,0:T(8,128)S(1)}, f32[3,10,8,128]{3,2,1,0:T(8,128)S(1)}, u32[]{:S(2)}, u32[]{:S(2)}) %collective-permute-start.4) | collective-permute-done | bytes 122912 | tf_op jit(solution)/shard_map/ppermute | solution.py:22
  31.5 0.0 collective-permute-done.5.from_below
  31.6 6.0 %collective-permute-start.6 = (f32[8,3,8,128]{3,2,1,0:T(8,128)S(1)}, f32[8,3,8,128]{3,2,1,0:T(8,128)S(1)}, u32[]{:S(2)}, u32[]{:S(2)}) collective-permute-start(f32[8,3,8,128]{3,2,1,0:T(8,128)S(1)} %get-tuple-element.35), channel_id=1, source_target_pairs={{0,31},{1,2},{2,1},{3,4},{4,3},{5,6},{6,5},{7,8},{8,7},{9,10},{10,... | collective-permute-start | bytes 294920 | tf_op jit(solution)/shard_map/ppermute | solution.py:28
  37.5 1.9 %collective-permute-start.7 = (f32[8,3,8,128]{3,2,1,0:T(8,128)S(1)}, f32[8,3,8,128]{3,2,1,0:T(8,128)S(1)}, u32[]{:S(2)}, u32[]{:S(2)}) collective-permute-start(f32[8,3,8,128]{3,2,1,0:T(8,128)S(1)} %get-tuple-element.36), channel_id=1, source_target_pairs={{0,1},{1,0},{2,3},{3,2},{4,5},{5,4},{6,7},{7,6},{8,9},{9,8},{10,11... | collective-permute-start | bytes 294920 | tf_op jit(solution)/shard_map/ppermute | solution.py:28
  39.5 0.7 %collective-permute-done.6.far_ref = f32[8,3,8,128]{3,2,1,0:T(8,128)S(1)} collective-permute-done((f32[8,3,8,128]{3,2,1,0:T(8,128)S(1)}, f32[8,3,8,128]{3,2,1,0:T(8,128)S(1)}, u32[]{:S(2)}, u32[]{:S(2)}) %collective-permute-start.6) | collective-permute-done | bytes 98336 | tf_op jit(solution)/shard_map/ppermute | solution.py:28
  40.1 3.9 %collective-permute-done.7.near_ref = f32[8,3,8,128]{3,2,1,0:T(8,128)S(1)} collective-permute-done((f32[8,3,8,128]{3,2,1,0:T(8,128)S(1)}, f32[8,3,8,128]{3,2,1,0:T(8,128)S(1)}, u32[]{:S(2)}, u32[]{:S(2)}) %collective-permute-start.7) | collective-permute-done | bytes 98336 | tf_op jit(solution)/shard_map/ppermute | solution.py:28
  44.0 1.3 %final.1 = f32[8,4,8,128]{3,2,1,0:T(8,128)} custom-call(f32[4]{0:T(128)S(1)} %copy-done.3, s32[8,4,128]{2,1,0:T(4,128)S(1)} %copy-done.1, f32[8,4,8,128]{3,2,1,0:T(8,128)S(1)} %get-tuple-element.30.own_ref, f32[8,3,8,128]{3,2,1,0:T(8,128)S(1)} %collective-permute-done.6.far_ref, f32[8,3,8,128]{3,2,1,0:T(8,128)S(1)} %collective-permute-done.7.near_ref, ...), custom_call_target="tpu_custom_call" | custom-call | tf_op jit(solution)/shard_map/final/pallas_call | solution.py:332
  (7 shorter events, 0.1 us)
Async XLA Ops:
  0.0 10.2 %collective-permute-start.1 = (s32[8,4,128]{2,1,0:T(4,128)}, s32[8,4,128]{2,1,0:T(4,128)S(1)}, u32[]{:S(2)}, u32[]{:S(2)}) collective-permute-start(s32[8,4,128]{2,1,0:T(4,128)} %classes_ref.1), channel_id=1, source_target_pairs={{0,31},{1,2},{2,1},{3,4},{4,3},{5,6},{6,5},{7,8},{8,7},{9,10},{10,... | collective-permute-start | bytes 49160 | tf_op jit(solution)/shard_map/ppermute | solution.py:28
  2.4 7.8 %collective-permute-start = (s32[8,4,128]{2,1,0:T(4,128)}, s32[8,4,128]{2,1,0:T(4,128)S(1)}, u32[]{:S(2)}, u32[]{:S(2)}) collective-permute-start(s32[8,4,128]{2,1,0:T(4,128)} %classes_ref.1), channel_id=1, source_target_pairs={{0,1},{1,0},{2,3},{3,2},{4,5},{5,4},{6,7},{7,6},{8,9},{9,8},{10,11... | collective-permute-start | bytes 49160 | tf_op jit(solution)/shard_map/ppermute | solution.py:28
  7.3 2.2 %copy-start = (f32[1024,1024]{1,0:T(8,128)S(1)}, f32[1024,1024]{1,0:T(8,128)}, u32[]{:S(2)}) copy-start(f32[1024,1024]{1,0:T(8,128)} %stiffness_ref.1) | copy-start | bytes 12582916
  9.5 0.7 %copy-start.1 = (s32[8,4,128]{2,1,0:T(4,128)S(1)}, s32[8,4,128]{2,1,0:T(4,128)}, u32[]{:S(2)}) copy-start(s32[8,4,128]{2,1,0:T(4,128)} %classes_ref.1) | copy-start | bytes 49156
  9.5 10.2 %copy-start.2 = (f32[8,128]{1,0:T(8,128)S(1)}, f32[8,128]{1,0:T(8,128)}, u32[]{:S(2)}) copy-start(f32[8,128]{1,0:T(8,128)} %coarse_ref.1) | copy-start | bytes 12292
  9.5 10.2 %copy-start.3 = (f32[4]{0:T(128)S(1)}, f32[4]{0:T(128)}, u32[]{:S(2)}) copy-start(f32[4]{0:T(128)} %contrast_ref.3) | copy-start | bytes 52
  10.3 9.4 %collective-permute-start.2 = (s32[9,4,128]{2,1,0:T(4,128)S(1)}, s32[9,4,128]{2,1,0:T(4,128)S(1)}, u32[]{:S(2)}, u32[]{:S(2)}) collective-permute-start(s32[9,4,128]{2,1,0:T(4,128)S(1)} %get-tuple-element.26), channel_id=1, source_target_pairs={{0,32},{32,64},{64,96},{96,128},{128,160},{160,192},{192,224},{224... | collective-permute-start | bytes 55304 | tf_op jit(solution)/shard_map/ppermute | solution.py:22
  10.3 9.4 %collective-permute-start.3 = (s32[9,4,128]{2,1,0:T(4,128)S(1)}, s32[9,4,128]{2,1,0:T(4,128)S(1)}, u32[]{:S(2)}, u32[]{:S(2)}) collective-permute-start(s32[9,4,128]{2,1,0:T(4,128)S(1)} %get-tuple-element.27), channel_id=1, source_target_pairs={{0,480},{32,0},{64,32},{96,64},{128,96},{160,128},{192,160},{224,1... | collective-permute-start | bytes 55304 | tf_op jit(solution)/shard_map/ppermute | solution.py:22
  26.0 5.5 %collective-permute-start.4 = (f32[3,10,8,128]{3,2,1,0:T(8,128)S(1)}, f32[3,10,8,128]{3,2,1,0:T(8,128)S(1)}, u32[]{:S(2)}, u32[]{:S(2)}) collective-permute-start(f32[3,10,8,128]{3,2,1,0:T(8,128)S(1)} %get-tuple-element.33), channel_id=1, source_target_pairs={{0,32},{32,64},{64,96},{96,128},{128,160},{160,192},{192,224},{224... | collective-permute-start | bytes 368648 | tf_op jit(solution)/shard_map/ppermute | solution.py:22
  26.0 5.5 %collective-permute-start.5 = (f32[3,10,8,128]{3,2,1,0:T(8,128)S(1)}, f32[3,10,8,128]{3,2,1,0:T(8,128)S(1)}, u32[]{:S(2)}, u32[]{:S(2)}) collective-permute-start(f32[3,10,8,128]{3,2,1,0:T(8,128)S(1)} %get-tuple-element.34), channel_id=1, source_target_pairs={{0,480},{32,0},{64,32},{96,64},{128,96},{160,128},{192,160},{224,1... | collective-permute-start | bytes 368648 | tf_op jit(solution)/shard_map/ppermute | solution.py:22
  31.6 8.5 %collective-permute-start.6 = (f32[8,3,8,128]{3,2,1,0:T(8,128)S(1)}, f32[8,3,8,128]{3,2,1,0:T(8,128)S(1)}, u32[]{:S(2)}, u32[]{:S(2)}) collective-permute-start(f32[8,3,8,128]{3,2,1,0:T(8,128)S(1)} %get-tuple-element.35), channel_id=1, source_target_pairs={{0,31},{1,2},{2,1},{3,4},{4,3},{5,6},{6,5},{7,8},{8,7},{9,10},{10,... | collective-permute-start | bytes 294920 | tf_op jit(solution)/shard_map/ppermute | solution.py:28
  37.5 6.5 %collective-permute-start.7 = (f32[8,3,8,128]{3,2,1,0:T(8,128)S(1)}, f32[8,3,8,128]{3,2,1,0:T(8,128)S(1)}, u32[]{:S(2)}, u32[]{:S(2)}) collective-permute-start(f32[8,3,8,128]{3,2,1,0:T(8,128)S(1)} %get-tuple-element.36), channel_id=1, source_target_pairs={{0,1},{1,0},{2,3},{3,2},{4,5},{5,4},{6,7},{7,6},{8,9},{9,8},{10,11... | collective-permute-start | bytes 294920 | tf_op jit(solution)/shard_map/ppermute | solution.py:28

commit v3 on v2

v3 whole, which is shorter than its diff:
```python
import functools

import jax
import jax.numpy as jnp
from jax import lax
from jax.experimental import pallas as pl
from jax.experimental.pallas import tpu as pltpu
from jax.sharding import PartitionSpec as P

SLOTS = 8
NGRP = 8
REACH = 3
NCLASS = 4
ITERS = 3
BF16 = jnp.bfloat16
F32 = jnp.float32


def moved(value, axis, steps):
    count = lax.axis_size(axis)
    pairs = [(source, (source + steps) % count) for source in range(count)]
    return lax.ppermute(value, axis, pairs)


def swapped(value, axis, first):
    count = lax.axis_size(axis)
    pairs = [(k, (((k - first) ^ 1) + first) % count) for k in range(count)]
    return lax.ppermute(value, axis, pairs)


def scale_of(classes, contrast_ref):
    value = jnp.full(classes.shape, contrast_ref[0], F32)
    for k in range(1, NCLASS):
        value = jnp.where(classes == k, contrast_ref[k], value)
    return jnp.sqrt(value)


def split(value):
    high = value.astype(BF16)
    return high, (value - high.astype(F32)).astype(BF16)


def product(left, right):
    return jnp.dot(left, right, preferred_element_type=F32)


def group_ones(width, group):
    row = lax.broadcasted_iota(jnp.int32, (width, width), 0) // group
    col = lax.broadcasted_iota(jnp.int32, (width, width), 1) // group
    return jnp.where(row == col, 1.0, 0.0).astype(BF16)


def places_of(index_x, index_y, places, row_count, col_count):
    block = (index_y >= col_count).astype(jnp.int32) + (index_y >= 2 * col_count)
    col = index_y - block * col_count
    deep = 2 * REACH
    return jnp.where(
        index_x < 0,
        places[3] + (block * deep + index_x + deep) * col_count + col,
        jnp.where(
            index_x >= row_count,
            places[4] + (block * deep + index_x - row_count) * col_count + col,
            (block * row_count + index_x) * col_count + col,
        ),
    )


def sides(near_ref, far_ref):
    even = lax.axis_index("yz") % 2 == 0
    near, far = near_ref[...], far_ref[...]
    return jnp.where(even, far, near), jnp.where(even, near, far)


def prepare_kernel(
    shift_x_ref, shift_y_ref, extent_ref, classes_ref, stiffness_ref,
    own_out, info_out, down_out, up_out, high_ref, low_ref,
    shift_x, shift_y, extent, landing, arrived, *, places,
):
    parts, part = landing.shape[:2]
    small = 64

    def copy(k):
        return pltpu.make_async_copy(
            stiffness_ref.at[pl.ds(k * part, part), :], landing.at[k], arrived.at[k]
        )

    others = [
        pltpu.make_async_copy(source, target, arrived.at[parts + k])
        for k, (source, target) in enumerate((
            (shift_x_ref, shift_x), (shift_y_ref, shift_y), (extent_ref, extent),
            (classes_ref, own_out),
        ))
    ]
    for other in others:
        other.start()
    for k in range(parts):
        copy(k).start()
    for other in others:
        other.wait()
    col_count, row_count = extent.shape
    shape = shift_x.shape
    slot = lax.broadcasted_iota(jnp.int32, shape, 0) + 1
    index_x = lax.broadcasted_iota(jnp.int32, shape, 2) + shift_x[...]
    index_y = lax.broadcasted_iota(jnp.int32, shape, 1) + shift_y[...] + col_count
    live = slot < extent[...][None]
    for out, move in ((info_out, 0), (down_out, -row_count), (up_out, row_count)):
        place = places_of(index_x + move, index_y, places, row_count, col_count)
        out[0] = extent[...]
        out[1:] = jnp.where(live, place, places[5])
    for k in range(parts):
        copy(k).wait()

        def step(j, carry):
            lines = pl.ds(pl.multiple_of(k * part + j * small, small), small)
            source = pl.ds(pl.multiple_of(j * small, small), small)
            high_ref[lines, :], low_ref[lines, :] = split(landing[k, source, :])
            return carry

        lax.fori_loop(0, part // small, step, 0)


def pack_kernel(far_ref, near_ref, own_ref, down_ref, up_ref, last_out, first_out, *, bound):
    left, right = sides(near_ref, far_ref)
    deep = 2 * REACH
    for k, block in enumerate((left, own_ref[...], right)):
        lines = slice(k * deep, (k + 1) * deep)
        last_out[lines] = block[block.shape[0] - deep:]
        first_out[lines] = block[:deep]
    for info_ref, out in ((down_ref, last_out), (up_ref, first_out)):
        places = info_ref[1:]
        reached = jnp.max((places < bound).astype(jnp.int32), axis=0)
        head = 3 * deep
        count = info_ref.shape[2]
        out[head:] = jnp.zeros((out.shape[0] - head,) + out.shape[1:], jnp.int32)
        out[head, :, :count] = info_ref[0] * reached
        out[head + 1:, :, :count] = places


def solve_kernel(
    info_ref, contrast_ref, near_ref, own_ref, far_ref, above_ref, below_ref, coarse_ref,
    high_ref, low_ref,
    own_out, far_out, near_out,
    scales, rows, start, spread, value, high, low, picture, weighted_high, weighted_low, total,
    ranks, *, row_count, col_count, dof, places,
):
    slots = SLOTS
    patches = row_count * col_count
    columns = coarse_ref.shape[0]
    own_place, bound, empty = places[1], places[3], places[5]
    deep = 2 * REACH
    ones = group_ones(2 * dof, dof // NGRP)
    small = ones[:dof, :dof]
    scales[...] = jnp.full(scales.shape, 1.0, F32)
    left, right = sides(near_ref, far_ref)
    for place, block in zip(places, (left, own_ref[...], right)):
        scales[pl.ds(place, patches), :] = scale_of(block, contrast_ref)
    for place, block in zip(places[3:], (above_ref, below_ref)):
        for x in range(3 * deep):
            scales[pl.ds(place + x * col_count, col_count), :] = scale_of(block[x], contrast_ref)
    inverse = 1.0 / scales[...]
    first, second = split(inverse * inverse)
    weight = product(first, small) + product(second, small)
    rows[...] = inverse * lax.rsqrt(weight)
    rows[pl.ds(empty, 8), :] = jnp.zeros((8, dof), F32)

    elements = [(r, y) for r in range(row_count + 2 * REACH) for y in range(col_count)]

    def first_place(r, y):
        x = r - REACH
        if x < 0:
            return places[3] + (deep + x + deep) * col_count + y
        if x >= row_count:
            return places[4] + (deep + x - row_count) * col_count + y
        return own_place + x * col_count + y

    width = 6
    half = 5

    def counted(extent, counters):
        late = extent >= half
        shift = jnp.where(late, extent - half, extent) * width
        step = jnp.left_shift(jnp.int32(1), shift)
        counter = jnp.where(late, counters[1], counters[0])
        held = jnp.bitwise_and(jnp.right_shift(counter, shift), (1 << width) - 1)
        none = jnp.int32(0)
        return held, (
            counters[0] + jnp.where(late, none, step), counters[1] + jnp.where(late, step, none)
        )

    counters = (jnp.int32(0), jnp.int32(0))
    for r, y in elements:
        _, counters = counted(info_ref[0, y, r], counters)
    starts = [jnp.int32(0), jnp.int32(0)]
    longer = [None] * (slots + 1)
    before = jnp.int32(0)
    for extent in range(slots, -1, -1):
        part, shift = divmod(extent, half)
        longer[extent] = before
        starts[part] = starts[part] + jnp.left_shift(before, shift * width)
        number = jnp.right_shift(counters[part], shift * width)
        before = before + jnp.bitwise_and(number, (1 << width) - 1)
    counters = tuple(starts)
    for p, (r, y) in enumerate(elements):
        rank, counters = counted(info_ref[0, y, r], counters)
        ranks[p] = rank
    for p, (r, y) in enumerate(elements):
        lines = pl.ds(pl.multiple_of(ranks[p] * columns, columns), columns)
        place = first_place(r, y)
        start[lines, :] = scales[place:place + 1, :] * coarse_ref[...]
        for k in range(slots):
            row = rows[pl.ds(place if k == 0 else info_ref[k, y, r], 1), :]
            spread[lines, k * dof:(k + 1) * dof] = jnp.broadcast_to(row, (columns, dof))

    block_rows = high.shape[1]
    pair = 2 * dof
    wide = 2 * pair

    def solve_block(b, pairs):
        lines = pl.ds(pl.multiple_of(b * block_rows, block_rows), block_rows)
        active = pairs * pair
        begin = start[lines, :]
        begin_high, begin_low = split(begin)
        for iteration in range(ITERS):
            for base in range(0, active, wide):
                lanes = slice(base, min(base + wide, active))
                if iteration == 0:
                    image = (
                        product(begin_high, high_ref[:dof, lanes])
                        + product(begin_high, low_ref[:dof, lanes])
                        + product(begin_low, high_ref[:dof, lanes])
                    )
                else:
                    source = (iteration - 1) % 2
                    image = (
                        product(high[source, :, :active], high_ref[:active, lanes])
                        + product(high[source, :, :active], low_ref[:active, lanes])
                        + product(low[source, :, :active], high_ref[:active, lanes])
                    )
                picture[:, lanes] = image
                first, second = split(spread[lines, lanes] * image)
                weighted_high[:, lanes] = first
                weighted_low[:, lanes] = second
            for base in range(0, active, pair):
                lanes = slice(base, base + pair)
                factor = spread[lines, lanes]
                mean = product(weighted_high[:, lanes], ones)
                mean = mean + product(weighted_low[:, lanes], ones)
                change = jnp.where(factor > 0.0, picture[:, lanes] - factor * mean, 0.0)
                result = -change if iteration == 0 else value[lines, lanes] - change
                value[lines, lanes] = result
                if iteration < ITERS - 1:
                    if base == 0:
                        result = jnp.concatenate(
                            [result[:, :dof] + begin, result[:, dof:]], axis=1
                        )
                    first, second = split(result)
                    high[iteration % 2, :, lanes] = first
                    low[iteration % 2, :, lanes] = second

    def solve_step(b, carry):
        passed = b * (block_rows // columns)
        pairs = jnp.int32(0)
        for k in range(slots // 2):
            pairs = pairs + jnp.where(longer[2 * k] > passed, 1, 0)
        for k in range(1, slots // 2 + 1):
            pl.when(pairs == k)(functools.partial(solve_block, b, k))
        return carry

    lax.fori_loop(0, spread.shape[0] // block_rows, solve_step, 0)

    total[...] = jnp.zeros(total.shape, F32)

    def result_of(p, k):
        lines = pl.ds(pl.multiple_of(ranks[p] * columns, columns), columns)
        return value[lines, k * dof:(k + 1) * dof]

    for p in range(patches):
        total[0, own_place + p] = result_of(p + REACH * col_count, 0)
    count = len(elements) // 2
    for q in range(count):
        sums = []
        for part in range(2):
            p = q + part * count
            r, y = elements[p]
            for k in range(1, slots):
                spot = jnp.minimum(info_ref[k, y, r], bound)
                sums.append((part, spot, total[part, spot] + result_of(p, k)))
        for part, spot, entry in sums:
            total[part, spot] = entry
    total[0] = total[0] + total[1]
    total = total.at[0]
    own_out[...] = total[pl.ds(own_place, patches)].reshape(own_out.shape)

    def store_sides(left_out, right_out):
        for x in range(row_count):
            for y in range(REACH):
                left_out[x, y] = total[places[0] + x * col_count + y + col_count - REACH]
                right_out[x, y] = total[places[2] + x * col_count + y]

    even = lax.axis_index("yz") % 2 == 0
    pl.when(even)(lambda: store_sides(far_out, near_out))
    pl.when(jnp.logical_not(even))(lambda: store_sides(near_out, far_out))


def final_kernel(contrast_ref, classes_ref, own_ref, far_ref, near_ref, out):
    count = own_ref.shape[1]
    reach = near_ref.shape[1]
    from_left, from_right = sides(near_ref, far_ref)
    inverse = 1.0 / scale_of(classes_ref[...], contrast_ref)
    out[...] = own_ref[...]
    out[:, count - reach:] = out[:, count - reach:] + from_right
    out[:, :reach] = out[:, :reach] + from_left
    out[...] = out[...] * inverse[:, :, None, :]


SMEM = pl.BlockSpec(memory_space=pltpu.SMEM)
VMEM = pl.BlockSpec(memory_space=pltpu.VMEM)


def grant(mebibytes):
    return pltpu.CompilerParams(vmem_limit_bytes=mebibytes * 1024 * 1024)


def shapes(*dims):
    return jax.ShapeDtypeStruct(dims, F32)


def per_device(classes, contrast, shift_x, shift_y, extent, coarse_basis, stiffness):
    row_count, col_count, dof = classes.shape
    columns = coarse_basis.shape[0]
    order = SLOTS * dof
    patches = row_count * col_count
    edge = 3 * 2 * REACH * col_count
    places = [0, patches, 2 * patches, 3 * patches, 3 * patches + edge, 3 * patches + 2 * edge]
    empty = places[5]

    far = swapped(classes, "yz", 1)
    near = swapped(classes, "yz", 0)

    stiff = jax.ShapeDtypeStruct((order, order), BF16)
    ends = jax.ShapeDtypeStruct((SLOTS, col_count, row_count), jnp.int32)
    parts = 8
    turned = (SLOTS - 1, col_count, row_count)
    sources = (
        shift_x.transpose(2, 1, 0), shift_y.transpose(2, 1, 0), extent.T, classes, stiffness
    )
    own, info, down, up, stiff_high, stiff_low = pl.pallas_call(
        functools.partial(prepare_kernel, places=places),
        in_specs=[pl.BlockSpec(memory_space=pltpu.HBM)] * 5,
        out_specs=[VMEM] * 6,
        out_shape=[
            jax.ShapeDtypeStruct(classes.shape, jnp.int32), ends, ends, ends, stiff, stiff
        ],
        scratch_shapes=[
            pltpu.VMEM(turned, jnp.int32),
            pltpu.VMEM(turned, jnp.int32),
            pltpu.VMEM(turned[1:], jnp.int32),
            pltpu.VMEM((parts, order // parts, order), F32),
            pltpu.SemaphoreType.DMA((parts + 4,)),
        ],
        compiler_params=grant(8),
        cost_estimate=pl.CostEstimate(
            flops=2 * order * order, bytes_accessed=8 * order * order, transcendentals=0
        ),
        name="prepare",
    )(*(pltpu.with_memory_space_constraint(source, pltpu.HBM) for source in sources))
    far, near, own, stiff_high, stiff_low, info, down, up = lax.optimization_barrier(
        (far, near, own, stiff_high, stiff_low, info, down, up)
    )
    head = 3 * 2 * REACH
    halo = jax.ShapeDtypeStruct((head + SLOTS, col_count, dof), jnp.int32)
    last_rows, first_rows = pl.pallas_call(
        functools.partial(pack_kernel, bound=places[3]),
        in_specs=[VMEM] * 5,
        out_specs=[VMEM] * 2,
        out_shape=[halo, halo],
        compiler_params=grant(4),
        name="pack",
    )(far, near, own, down, up)
    above = moved(last_rows, "gx", 1)
    below = moved(first_rows, "gx", -1)

    info = jnp.concatenate(
        [above[head:, :, row_count - REACH:row_count], info, below[head:, :, :REACH]], axis=2
    )
    whole = (row_count, col_count, columns, dof)
    side = shapes(row_count, REACH, columns, dof)
    total_rows = (row_count + 2 * REACH) * col_count * columns
    block_rows = total_rows // 2
    own_sum, far_sum, near_sum = pl.pallas_call(
        functools.partial(
            solve_kernel, row_count=row_count, col_count=col_count, dof=dof, places=places
        ),
        in_specs=[SMEM, SMEM] + [VMEM] * 8,
        out_specs=[VMEM] * 3,
        out_shape=[shapes(*whole), side, side],
        scratch_shapes=[
            pltpu.VMEM((empty + 8, dof), F32),
            pltpu.VMEM((empty + 8, dof), F32),
            pltpu.VMEM((total_rows, dof), F32),
            pltpu.VMEM((total_rows, order), F32),
            pltpu.VMEM((total_rows, order), F32),
            pltpu.VMEM((2, block_rows, order), BF16),
            pltpu.VMEM((2, block_rows, order), BF16),
            pltpu.VMEM((block_rows, order), F32),
            pltpu.VMEM((block_rows, order), BF16),
            pltpu.VMEM((block_rows, order), BF16),
            pltpu.VMEM((2, places[3] + 1, columns, dof), F32),
            pltpu.SMEM((64,), jnp.int32),
        ],
        compiler_params=grant(16),
        name="solve",
    )(
        info, contrast, near.reshape(patches, dof), own.reshape(patches, dof),
        far.reshape(patches, dof), above, below, coarse_basis, stiff_high, stiff_low,
    )
    far_sum = swapped(far_sum, "yz", 1)
    near_sum = swapped(near_sum, "yz", 0)
    return pl.pallas_call(
        final_kernel,
        in_specs=[SMEM] + [VMEM] * 4,
        out_specs=VMEM,
        out_shape=shapes(*whole),
        compiler_params=grant(4),
        name="final",
    )(contrast, own, own_sum, far_sum, near_sum)


def solution(mesh):
    return jax.shard_map(
        per_device,
        mesh=mesh,
        in_specs=(
            P("gx", "yz", None),
            P(),
            P("gx", "yz", None),
            P("gx", "yz", None),
            P("gx", "yz"),
            P(),
            P(),
        ),
        out_specs=P("gx", "yz", None, None),
        check_vma=False,
    )
```

time: 45.7 us -> 43.2 us (0.945)
  Pallas kernels: 8.28 us -> 12.7 us
  waiting for transfers between devices: 8.6 us -> 6.38 us
  local copies, waits for them, and re-layouts: 2.19 us -> 0.08 us
  starting transfers between devices: 25.3 us -> 23.6 us
  other arithmetic: 0.81 us -> 0.08 us
    ppermute x4 -> x2, starting transfers between devices: 10.9 us -> 7.95 us  [moved(): return lax.ppermute(value, axis, pairs)]
    pallas_call x1, Pallas kernels: 6.28 us -> 9.03 us  [per_device(): pl.pallas_call(functools.partial(solve_kernel, row_count=row_count, col_c...]
    ppermute x4 -> x2, waiting for transfers between devices: 4.01 us -> 1.8 us  [moved(): return lax.ppermute(value, axis, pairs)]
    unnamed x8 -> x4, local copies, waits for them, and re-layouts: 2.19 us -> 0.01 us
    pallas_call x4 -> x3, Pallas kernels: 2 us -> 3.69 us  [the longest x1 2.41 us: per_device(): pl.pallas_call(functools.partial(prepare_kernel, places=places), in_specs...]
    ppermute x4, starting transfers between devices: 14.4 us -> 15.7 us  [swapped(): return lax.ppermute(value, axis, pairs)]
    select_n x1 -> x0, other arithmetic: 0.81 us -> none  [index_of(): return jnp.where(slot < extent, index, places[5])]
  transfers between devices with their start and end apart: 8 -> 6, of which waited for: 4 -> 3; matrix products, arithmetic and copies ran while one was open for 2% -> 0% of each run, Pallas kernels for 2% -> 6%
where the time goes in v3:
time: 43.2 us; the launch traced here: 43 us
  starting transfers between devices  23.6 us (55%)
  Pallas kernels  12.7 us (29%)
  waiting for transfers between devices  6.38 us (15%)
    ppermute x4, starting transfers between devices, swapped(): return lax.ppermute(value, axis, pairs)  15.7 us
    pallas_call x1, Pallas kernels, per_device(): pl.pallas_call(functools.partial(solve_kernel, row_count=row_count, col_c...  9.03 us
    ppermute x2, starting transfers between devices, moved(): return lax.ppermute(value, axis, pairs)  7.95 us
    ppermute x4, waiting for transfers between devices, swapped(): return lax.ppermute(value, axis, pairs)  4.59 us
    pallas_call x1, Pallas kernels, per_device(): pl.pallas_call(functools.partial(prepare_kernel, places=places), in_specs...  2.41 us
    ppermute x2, waiting for transfers between devices, moved(): return lax.ppermute(value, axis, pairs)  1.8 us
    pallas_call x1, Pallas kernels, per_device(): pl.pallas_call(final_kernel, in_specs=[SMEM] + [VMEM] * 4, out_specs=VMEM...  1.25 us
  transfers between devices with their start and end apart: 6, of which 3 were waited for; matrix products, arithmetic and copies ran while one was open for 0% of the time, Pallas kernels for 6%

profile of v3, /device:TPU:4, one launch (start us, length us, event | category | flops | bytes accessed | tf_op | source)
XLA Modules:
  0.0 43.0 jit_solution(17482604058879219402)
XLA Ops:
  0.0 2.4 %collective-permute-start = (s32[8,4,128]{2,1,0:T(4,128)}, s32[8,4,128]{2,1,0:T(4,128)S(1)}, u32[]{:S(2)}, u32[]{:S(2)}) collective-permute-start(s32[8,4,128]{2,1,0:T(4,128)} %classes_ref.1), channel_id=1, source_target_pairs={{0,31},{1,2},{2,1},{3,4},{4,3},{5,6},{6,5},{7,8},{8,7},{9,10},{10,... | collective-permute-start | bytes 49160 | tf_op jit(solution)/shard_map/ppermute | solution.py:28
  2.4 4.1 %collective-permute-start.1 = (s32[8,4,128]{2,1,0:T(4,128)}, s32[8,4,128]{2,1,0:T(4,128)S(1)}, u32[]{:S(2)}, u32[]{:S(2)}) collective-permute-start(s32[8,4,128]{2,1,0:T(4,128)} %classes_ref.1), channel_id=1, source_target_pairs={{0,1},{1,0},{2,3},{3,2},{4,5},{5,4},{6,7},{7,6},{8,9},{9,8},{10,11... | collective-permute-start | bytes 49160 | tf_op jit(solution)/shard_map/ppermute | solution.py:28
  6.5 0.0 copy-start
  6.5 0.0 copy-start.1
  6.5 2.4 %prepare.1 = (s32[8,4,128]{2,1,0:T(4,128)S(1)}, s32[8,4,8]{2,1,0:T(4,128)S(1)}, s32[8,4,8]{2,1,0:T(4,128)S(1)}, s32[8,4,8]{2,1,0:T(4,128)S(1)}, bf16[1024,1024]{...) custom-call(s32[7,4,8]{2,1,0:T(4,128)} %bitcast.9, s32[7,4,8]{2,1,0:T(4,128)} %bitcast.10, s32[4,8]{1,0:T(4,128)} %bitcast.11, ...), custom_call_target="tpu_custom_call" | custom-call | flops 2097152 | bytes 8388608 | tf_op jit(solution)/shard_map/prepare/pallas_call | solution.py:347
  8.9 0.0 collective-permute-done.far_ref
  9.0 0.0 collective-permute-done.1.near_ref
  9.0 0.0 collective-permute-start.2
  9.0 7.9 %collective-permute-start.3 = (s32[26,4,128]{2,1,0:T(4,128)S(1)}, s32[26,4,128]{2,1,0:T(4,128)S(1)}, u32[]{:S(2)}, u32[]{:S(2)}) collective-permute-start(s32[26,4,128]{2,1,0:T(4,128)S(1)} %get-tuple-element.37), channel_id=1, source_target_pairs={{0,480},{32,0},{64,32},{96,64},{128,96},{160,128},{192,160},{224,1... | collective-permute-start | bytes 159752 | tf_op jit(solution)/shard_map/ppermute | solution.py:22
  17.0 1.8 %collective-permute-done.2.above_ref = s32[26,4,128]{2,1,0:T(4,128)S(1)} collective-permute-done((s32[26,4,128]{2,1,0:T(4,128)S(1)}, s32[26,4,128]{2,1,0:T(4,128)S(1)}, u32[]{:S(2)}, u32[]{:S(2)}) %collective-permute-start.2) | collective-permute-done | bytes 53280 | tf_op jit(solution)/shard_map/ppermute | solution.py:22
  18.8 0.1 slice.8
  18.8 0.0 collective-permute-done.3.below_ref
  18.8 0.1 pad_add_fusion.info_ref
  18.9 0.0 copy-done
  18.9 0.0 copy-done.1
  19.0 9.0 %solve.1 = (f32[8,4,8,128]{3,2,1,0:T(8,128)S(1)}, f32[8,3,8,128]{3,2,1,0:T(8,128)S(1)}, f32[8,3,8,128]{3,2,1,0:T(8,128)S(1)}) custom-call(s32[8,4,14]{2,1,0:T(4,128)S(1)} %pad_add_fusion.info_ref, f32[4]{0:T(128)S(1)} %copy-done.1, s32[32,128]{1,0:T(8,128)S(1)} %bitcast.8, s32[32,128]{1,0:T(8,128)S(1)} %bitcast.6, s32[32,128]{1,0:T(8,128)S(1)} %bitcast.7, ...), custom_call_target="tpu_custom_call" | custom-call | tf_op jit(solution)/shard_map/solve/pallas_call | solution.py:390
  28.0 7.3 %collective-permute-start.4 = (f32[8,3,8,128]{3,2,1,0:T(8,128)S(1)}, f32[8,3,8,128]{3,2,1,0:T(8,128)S(1)}, u32[]{:S(2)}, u32[]{:S(2)}) collective-permute-start(f32[8,3,8,128]{3,2,1,0:T(8,128)S(1)} %get-tuple-element.41), channel_id=1, source_target_pairs={{0,31},{1,2},{2,1},{3,4},{4,3},{5,6},{6,5},{7,8},{8,7},{9,10},{10,... | collective-permute-start | bytes 294920 | tf_op jit(solution)/shard_map/ppermute | solution.py:28
  35.2 1.9 %collective-permute-start.5 = (f32[8,3,8,128]{3,2,1,0:T(8,128)S(1)}, f32[8,3,8,128]{3,2,1,0:T(8,128)S(1)}, u32[]{:S(2)}, u32[]{:S(2)}) collective-permute-start(f32[8,3,8,128]{3,2,1,0:T(8,128)S(1)} %get-tuple-element.42), channel_id=1, source_target_pairs={{0,1},{1,0},{2,3},{3,2},{4,5},{5,4},{6,7},{7,6},{8,9},{9,8},{10,11... | collective-permute-start | bytes 294920 | tf_op jit(solution)/shard_map/ppermute | solution.py:28
  37.2 0.7 %collective-permute-done.4.far_ref = f32[8,3,8,128]{3,2,1,0:T(8,128)S(1)} collective-permute-done((f32[8,3,8,128]{3,2,1,0:T(8,128)S(1)}, f32[8,3,8,128]{3,2,1,0:T(8,128)S(1)}, u32[]{:S(2)}, u32[]{:S(2)}) %collective-permute-start.4) | collective-permute-done | bytes 98336 | tf_op jit(solution)/shard_map/ppermute | solution.py:28
  37.8 3.9 %collective-permute-done.5.near_ref = f32[8,3,8,128]{3,2,1,0:T(8,128)S(1)} collective-permute-done((f32[8,3,8,128]{3,2,1,0:T(8,128)S(1)}, f32[8,3,8,128]{3,2,1,0:T(8,128)S(1)}, u32[]{:S(2)}, u32[]{:S(2)}) %collective-permute-start.5) | collective-permute-done | bytes 98336 | tf_op jit(solution)/shard_map/ppermute | solution.py:28
  41.8 1.2 %final.1 = f32[8,4,8,128]{3,2,1,0:T(8,128)} custom-call(f32[4]{0:T(128)S(1)} %copy-done.1, s32[8,4,128]{2,1,0:T(4,128)S(1)} %get-tuple-element.30.own_ref.classes_ref, f32[8,4,8,128]{3,2,1,0:T(8,128)S(1)} %get-tuple-element.40.own_ref, f32[8,3,8,128]{3,2,1,0:T(8,128)S(1)} %collective-permute-done.4.far_ref, f32[8,3,8,128]{3,2,1,0:T(8,128)S(1)} %collective-permute-done.5.near_ref), custom_call_target="tpu_custom_call" | custom-call | tf_op jit(solution)/shard_map/final/pallas_call | solution.py:419
  (2 shorter events, 0.0 us)
Async XLA Ops:
  0.0 9.0 %collective-permute-start = (s32[8,4,128]{2,1,0:T(4,128)}, s32[8,4,128]{2,1,0:T(4,128)S(1)}, u32[]{:S(2)}, u32[]{:S(2)}) collective-permute-start(s32[8,4,128]{2,1,0:T(4,128)} %classes_ref.1), channel_id=1, source_target_pairs={{0,31},{1,2},{2,1},{3,4},{4,3},{5,6},{6,5},{7,8},{8,7},{9,10},{10,... | collective-permute-start | bytes 49160 | tf_op jit(solution)/shard_map/ppermute | solution.py:28
  2.4 6.5 %collective-permute-start.1 = (s32[8,4,128]{2,1,0:T(4,128)}, s32[8,4,128]{2,1,0:T(4,128)S(1)}, u32[]{:S(2)}, u32[]{:S(2)}) collective-permute-start(s32[8,4,128]{2,1,0:T(4,128)} %classes_ref.1), channel_id=1, source_target_pairs={{0,1},{1,0},{2,3},{3,2},{4,5},{5,4},{6,7},{7,6},{8,9},{9,8},{10,11... | collective-permute-start | bytes 49160 | tf_op jit(solution)/shard_map/ppermute | solution.py:28
  6.5 12.4 %copy-start = (f32[8,128]{1,0:T(8,128)S(1)}, f32[8,128]{1,0:T(8,128)}, u32[]{:S(2)}) copy-start(f32[8,128]{1,0:T(8,128)} %coarse_ref.1) | copy-start | bytes 12292
  6.5 12.4 %copy-start.1 = (f32[4]{0:T(128)S(1)}, f32[4]{0:T(128)}, u32[]{:S(2)}) copy-start(f32[4]{0:T(128)} %contrast_ref.3) | copy-start | bytes 52
  9.0 9.8 %collective-permute-start.2 = (s32[26,4,128]{2,1,0:T(4,128)S(1)}, s32[26,4,128]{2,1,0:T(4,128)S(1)}, u32[]{:S(2)}, u32[]{:S(2)}) collective-permute-start(s32[26,4,128]{2,1,0:T(4,128)S(1)} %get-tuple-element.35), channel_id=1, source_target_pairs={{0,32},{32,64},{64,96},{96,128},{128,160},{160,192},{192,224},{224... | collective-permute-start | bytes 159752 | tf_op jit(solution)/shard_map/ppermute | solution.py:22
  9.0 9.8 %collective-permute-start.3 = (s32[26,4,128]{2,1,0:T(4,128)S(1)}, s32[26,4,128]{2,1,0:T(4,128)S(1)}, u32[]{:S(2)}, u32[]{:S(2)}) collective-permute-start(s32[26,4,128]{2,1,0:T(4,128)S(1)} %get-tuple-element.37), channel_id=1, source_target_pairs={{0,480},{32,0},{64,32},{96,64},{128,96},{160,128},{192,160},{224,1... | collective-permute-start | bytes 159752 | tf_op jit(solution)/shard_map/ppermute | solution.py:22
  28.0 9.8 %collective-permute-start.4 = (f32[8,3,8,128]{3,2,1,0:T(8,128)S(1)}, f32[8,3,8,128]{3,2,1,0:T(8,128)S(1)}, u32[]{:S(2)}, u32[]{:S(2)}) collective-permute-start(f32[8,3,8,128]{3,2,1,0:T(8,128)S(1)} %get-tuple-element.41), channel_id=1, source_target_pairs={{0,31},{1,2},{2,1},{3,4},{4,3},{5,6},{6,5},{7,8},{8,7},{9,10},{10,... | collective-permute-start | bytes 294920 | tf_op jit(solution)/shard_map/ppermute | solution.py:28
  35.2 6.5 %collective-permute-start.5 = (f32[8,3,8,128]{3,2,1,0:T(8,128)S(1)}, f32[8,3,8,128]{3,2,1,0:T(8,128)S(1)}, u32[]{:S(2)}, u32[]{:S(2)}) collective-permute-start(f32[8,3,8,128]{3,2,1,0:T(8,128)S(1)} %get-tuple-element.42), channel_id=1, source_target_pairs={{0,1},{1,0},{2,3},{3,2},{4,5},{5,4},{6,7},{7,6},{8,9},{9,8},{10,11... | collective-permute-start | bytes 294920 | tf_op jit(solution)/shard_map/ppermute | solution.py:28

commit v4 on v3

--- a/solution.py
+++ b/solution.py
@@ -139,7 +139,7 @@
 def solve_kernel(
     info_ref, contrast_ref, near_ref, own_ref, far_ref, above_ref, below_ref, coarse_ref,
     high_ref, low_ref,
-    own_out, far_out, near_out,
+    own_out, far_out, near_out, inverse_out,
     scales, rows, start, spread, value, high, low, picture, weighted_high, weighted_low, total,
     ranks, *, row_count, col_count, dof, places,
 ):
@@ -161,6 +161,7 @@
     first, second = split(inverse * inverse)
     weight = product(first, small) + product(second, small)
     rows[...] = inverse * lax.rsqrt(weight)
+    inverse_out[...] = inverse[own_place:own_place + patches].reshape(inverse_out.shape)
     rows[pl.ds(empty, 8), :] = jnp.zeros((8, dof), F32)
 
     elements = [(r, y) for r in range(row_count + 2 * REACH) for y in range(col_count)]
@@ -302,15 +303,14 @@
     pl.when(jnp.logical_not(even))(lambda: store_sides(near_out, far_out))
 
 
-def final_kernel(contrast_ref, classes_ref, own_ref, far_ref, near_ref, out):
+def final_kernel(inverse_ref, own_ref, far_ref, near_ref, out):
     count = own_ref.shape[1]
     reach = near_ref.shape[1]
     from_left, from_right = sides(near_ref, far_ref)
-    inverse = 1.0 / scale_of(classes_ref[...], contrast_ref)
     out[...] = own_ref[...]
     out[:, count - reach:] = out[:, count - reach:] + from_right
     out[:, :reach] = out[:, :reach] + from_left
-    out[...] = out[...] * inverse[:, :, None, :]
+    out[...] = out[...] * inverse_ref[...][:, :, None, :]
 
 
 SMEM = pl.BlockSpec(memory_space=pltpu.SMEM)
@@ -387,13 +387,13 @@
     side = shapes(row_count, REACH, columns, dof)
     total_rows = (row_count + 2 * REACH) * col_count * columns
     block_rows = total_rows // 2
-    own_sum, far_sum, near_sum = pl.pallas_call(
+    own_sum, far_sum, near_sum, inverse = pl.pallas_call(
         functools.partial(
             solve_kernel, row_count=row_count, col_count=col_count, dof=dof, places=places
         ),
         in_specs=[SMEM, SMEM] + [VMEM] * 8,
-        out_specs=[VMEM] * 3,
-        out_shape=[shapes(*whole), side, side],
+        out_specs=[VMEM] * 4,
+        out_shape=[shapes(*whole), side, side, shapes(row_count, col_count, dof)],
         scratch_shapes=[
             pltpu.VMEM((empty + 8, dof), F32),
             pltpu.VMEM((empty + 8, dof), F32),
@@ -418,12 +418,12 @@
     near_sum = swapped(near_sum, "yz", 0)
     return pl.pallas_call(
         final_kernel,
-        in_specs=[SMEM] + [VMEM] * 4,
+        in_specs=[VMEM] * 4,
         out_specs=VMEM,
         out_shape=shapes(*whole),
         compiler_params=grant(4),
         name="final",
-    )(contrast, own, own_sum, far_sum, near_sum)
+    )(inverse, own_sum, far_sum, near_sum)
 
 
 def solution(mesh):

time: 43.2 us -> 41.9 us (0.970)
  the two profiles are of different devices: /device:TPU:4 before, /device:TPU:193 now
where the time goes in v4:
time: 41.9 us; the launch traced here: 41.6 us
  starting transfers between devices  20.8 us (50%)
  Pallas kernels  12.2 us (29%)
  waiting for transfers between devices  8.44 us (20%)
    ppermute x4, starting transfers between devices, swapped(): return lax.ppermute(value, axis, pairs)  15.5 us
    pallas_call x1, Pallas kernels, per_device(): pl.pallas_call(functools.partial(solve_kernel, row_count=row_count, col_c...  9.02 us
    ppermute x2, starting transfers between devices, moved(): return lax.ppermute(value, axis, pairs)  5.31 us
    ppermute x2, waiting for transfers between devices, moved(): return lax.ppermute(value, axis, pairs)  4.69 us
    ppermute x4, waiting for transfers between devices, swapped(): return lax.ppermute(value, axis, pairs)  3.75 us
    pallas_call x1, Pallas kernels, per_device(): pl.pallas_call(functools.partial(prepare_kernel, places=places), in_specs...  2.41 us
  transfers between devices with their start and end apart: 6, of which 5 were waited for; matrix products, arithmetic and copies ran while one was open for 0% of the time, Pallas kernels for 6%

profile of v4, /device:TPU:193, one launch (start us, length us, event | category | flops | bytes accessed | tf_op | source)
XLA Modules:
  0.0 41.6 jit_solution(15415766551635580952)
XLA Ops:
  0.0 7.3 %collective-permute-start = (s32[8,4,128]{2,1,0:T(4,128)}, s32[8,4,128]{2,1,0:T(4,128)S(1)}, u32[]{:S(2)}, u32[]{:S(2)}) collective-permute-start(s32[8,4,128]{2,1,0:T(4,128)} %classes_ref.1), channel_id=1, source_target_pairs={{0,31},{1,2},{2,1},{3,4},{4,3},{5,6},{6,5},{7,8},{8,7},{9,10},{10,... | collective-permute-start | bytes 49160 | tf_op jit(solution)/shard_map/ppermute | solution.py:28
  7.3 1.9 %collective-permute-start.1 = (s32[8,4,128]{2,1,0:T(4,128)}, s32[8,4,128]{2,1,0:T(4,128)S(1)}, u32[]{:S(2)}, u32[]{:S(2)}) collective-permute-start(s32[8,4,128]{2,1,0:T(4,128)} %classes_ref.1), channel_id=1, source_target_pairs={{0,1},{1,0},{2,3},{3,2},{4,5},{5,4},{6,7},{7,6},{8,9},{9,8},{10,11... | collective-permute-start | bytes 49160 | tf_op jit(solution)/shard_map/ppermute | solution.py:28
  9.2 0.0 copy-start
  9.2 0.0 copy-start.1
  9.2 2.4 %prepare.1 = (s32[8,4,128]{2,1,0:T(4,128)S(1)}, s32[8,4,8]{2,1,0:T(4,128)S(1)}, s32[8,4,8]{2,1,0:T(4,128)S(1)}, s32[8,4,8]{2,1,0:T(4,128)S(1)}, bf16[1024,1024]{...) custom-call(s32[7,4,8]{2,1,0:T(4,128)} %bitcast.9, s32[7,4,8]{2,1,0:T(4,128)} %bitcast.10, s32[4,8]{1,0:T(4,128)} %bitcast.11, ...), custom_call_target="tpu_custom_call" | custom-call | flops 2097152 | bytes 8388608 | tf_op jit(solution)/shard_map/prepare/pallas_call | solution.py:347
  11.7 0.0 collective-permute-done.far_ref
  11.7 0.3 collective-permute-done.1.near_ref
  12.0 5.3 %collective-permute-start.2 = (s32[26,4,128]{2,1,0:T(4,128)S(1)}, s32[26,4,128]{2,1,0:T(4,128)S(1)}, u32[]{:S(2)}, u32[]{:S(2)}) collective-permute-start(s32[26,4,128]{2,1,0:T(4,128)S(1)} %get-tuple-element.36), channel_id=1, source_target_pairs={{0,32},{32,64},{64,96},{96,128},{128,160},{160,192},{192,224},{224... | collective-permute-start | bytes 159752 | tf_op jit(solution)/shard_map/ppermute | solution.py:22
  17.3 0.0 collective-permute-start.3
  17.3 1.2 %collective-permute-done.2.above_ref = s32[26,4,128]{2,1,0:T(4,128)S(1)} collective-permute-done((s32[26,4,128]{2,1,0:T(4,128)S(1)}, s32[26,4,128]{2,1,0:T(4,128)S(1)}, u32[]{:S(2)}, u32[]{:S(2)}) %collective-permute-start.2) | collective-permute-done | bytes 53280 | tf_op jit(solution)/shard_map/ppermute | solution.py:22
  18.5 0.1 slice.8
  18.6 3.5 %collective-permute-done.3.below_ref = s32[26,4,128]{2,1,0:T(4,128)S(1)} collective-permute-done((s32[26,4,128]{2,1,0:T(4,128)S(1)}, s32[26,4,128]{2,1,0:T(4,128)S(1)}, u32[]{:S(2)}, u32[]{:S(2)}) %collective-permute-start.3) | collective-permute-done | bytes 53280 | tf_op jit(solution)/shard_map/ppermute | solution.py:22
  22.1 0.1 pad_add_fusion.info_ref
  22.2 0.0 copy-done
  22.2 0.0 copy-done.1
  22.2 9.0 %solve.1 = (f32[8,4,8,128]{3,2,1,0:T(8,128)S(1)}, f32[8,3,8,128]{3,2,1,0:T(8,128)S(1)}, f32[8,3,8,128]{3,2,1,0:T(8,128)S(1)}, f32[8,4,128]{2,1,0:T(4,128)S(1)}) custom-call(s32[8,4,14]{2,1,0:T(4,128)S(1)} %pad_add_fusion.info_ref, f32[4]{0:T(128)S(1)} %copy-done.1, s32[32,128]{1,0:T(8,128)S(1)} %bitcast.7, s32[32,128]{1,0:T(8,128)S(1)} %bitcast.8, ...), custom_call_target="tpu_custom_call" | custom-call | tf_op jit(solution)/shard_map/solve/pallas_call | solution.py:390
  31.2 4.4 %collective-permute-start.4 = (f32[8,3,8,128]{3,2,1,0:T(8,128)S(1)}, f32[8,3,8,128]{3,2,1,0:T(8,128)S(1)}, u32[]{:S(2)}, u32[]{:S(2)}) collective-permute-start(f32[8,3,8,128]{3,2,1,0:T(8,128)S(1)} %get-tuple-element.43), channel_id=1, source_target_pairs={{0,31},{1,2},{2,1},{3,4},{4,3},{5,6},{6,5},{7,8},{8,7},{9,10},{10,... | collective-permute-start | bytes 294920 | tf_op jit(solution)/shard_map/ppermute | solution.py:28
  35.6 1.9 %collective-permute-start.5 = (f32[8,3,8,128]{3,2,1,0:T(8,128)S(1)}, f32[8,3,8,128]{3,2,1,0:T(8,128)S(1)}, u32[]{:S(2)}, u32[]{:S(2)}) collective-permute-start(f32[8,3,8,128]{3,2,1,0:T(8,128)S(1)} %get-tuple-element.44), channel_id=1, source_target_pairs={{0,1},{1,0},{2,3},{3,2},{4,5},{5,4},{6,7},{7,6},{8,9},{9,8},{10,11... | collective-permute-start | bytes 294920 | tf_op jit(solution)/shard_map/ppermute | solution.py:28
  37.5 2.4 %collective-permute-done.4.far_ref = f32[8,3,8,128]{3,2,1,0:T(8,128)S(1)} collective-permute-done((f32[8,3,8,128]{3,2,1,0:T(8,128)S(1)}, f32[8,3,8,128]{3,2,1,0:T(8,128)S(1)}, u32[]{:S(2)}, u32[]{:S(2)}) %collective-permute-start.4) | collective-permute-done | bytes 98336 | tf_op jit(solution)/shard_map/ppermute | solution.py:28
  39.9 1.0 %collective-permute-done.5.near_ref = f32[8,3,8,128]{3,2,1,0:T(8,128)S(1)} collective-permute-done((f32[8,3,8,128]{3,2,1,0:T(8,128)S(1)}, f32[8,3,8,128]{3,2,1,0:T(8,128)S(1)}, u32[]{:S(2)}, u32[]{:S(2)}) %collective-permute-start.5) | collective-permute-done | bytes 98336 | tf_op jit(solution)/shard_map/ppermute | solution.py:28
  40.9 0.7 %final.1 = f32[8,4,8,128]{3,2,1,0:T(8,128)} custom-call(f32[8,4,128]{2,1,0:T(4,128)S(1)} %get-tuple-element.41.inverse_ref, f32[8,4,8,128]{3,2,1,0:T(8,128)S(1)} %get-tuple-element.42.own_ref, f32[8,3,8,128]{3,2,1,0:T(8,128)S(1)} %collective-permute-done.4.far_ref, f32[8,3,8,128]{3,2,1,0:T(8,128)S(1)} %collective-permute-done.5.near_ref), custom_call_target="tpu_custom_call" | custom-call | tf_op jit(solution)/shard_map/final/pallas_call | solution.py:419
  (2 shorter events, 0.0 us)
Async XLA Ops:
  0.0 11.7 %collective-permute-start = (s32[8,4,128]{2,1,0:T(4,128)}, s32[8,4,128]{2,1,0:T(4,128)S(1)}, u32[]{:S(2)}, u32[]{:S(2)}) collective-permute-start(s32[8,4,128]{2,1,0:T(4,128)} %classes_ref.1), channel_id=1, source_target_pairs={{0,31},{1,2},{2,1},{3,4},{4,3},{5,6},{6,5},{7,8},{8,7},{9,10},{10,... | collective-permute-start | bytes 49160 | tf_op jit(solution)/shard_map/ppermute | solution.py:28
  7.3 4.7 %collective-permute-start.1 = (s32[8,4,128]{2,1,0:T(4,128)}, s32[8,4,128]{2,1,0:T(4,128)S(1)}, u32[]{:S(2)}, u32[]{:S(2)}) collective-permute-start(s32[8,4,128]{2,1,0:T(4,128)} %classes_ref.1), channel_id=1, source_target_pairs={{0,1},{1,0},{2,3},{3,2},{4,5},{5,4},{6,7},{7,6},{8,9},{9,8},{10,11... | collective-permute-start | bytes 49160 | tf_op jit(solution)/shard_map/ppermute | solution.py:28
  9.2 13.0 %copy-start = (f32[8,128]{1,0:T(8,128)S(1)}, f32[8,128]{1,0:T(8,128)}, u32[]{:S(2)}) copy-start(f32[8,128]{1,0:T(8,128)} %coarse_ref.1) | copy-start | bytes 12292
  9.2 13.0 %copy-start.1 = (f32[4]{0:T(128)S(1)}, f32[4]{0:T(128)}, u32[]{:S(2)}) copy-start(f32[4]{0:T(128)} %contrast_ref.1) | copy-start | bytes 52
  12.0 6.5 %collective-permute-start.2 = (s32[26,4,128]{2,1,0:T(4,128)S(1)}, s32[26,4,128]{2,1,0:T(4,128)S(1)}, u32[]{:S(2)}, u32[]{:S(2)}) collective-permute-start(s32[26,4,128]{2,1,0:T(4,128)S(1)} %get-tuple-element.36), channel_id=1, source_target_pairs={{0,32},{32,64},{64,96},{96,128},{128,160},{160,192},{192,224},{224... | collective-permute-start | bytes 159752 | tf_op jit(solution)/shard_map/ppermute | solution.py:22
  17.3 4.8 %collective-permute-start.3 = (s32[26,4,128]{2,1,0:T(4,128)S(1)}, s32[26,4,128]{2,1,0:T(4,128)S(1)}, u32[]{:S(2)}, u32[]{:S(2)}) collective-permute-start(s32[26,4,128]{2,1,0:T(4,128)S(1)} %get-tuple-element.38), channel_id=1, source_target_pairs={{0,480},{32,0},{64,32},{96,64},{128,96},{160,128},{192,160},{224,1... | collective-permute-start | bytes 159752 | tf_op jit(solution)/shard_map/ppermute | solution.py:22
  31.2 8.7 %collective-permute-start.4 = (f32[8,3,8,128]{3,2,1,0:T(8,128)S(1)}, f32[8,3,8,128]{3,2,1,0:T(8,128)S(1)}, u32[]{:S(2)}, u32[]{:S(2)}) collective-permute-start(f32[8,3,8,128]{3,2,1,0:T(8,128)S(1)} %get-tuple-element.43), channel_id=1, source_target_pairs={{0,31},{1,2},{2,1},{3,4},{4,3},{5,6},{6,5},{7,8},{8,7},{9,10},{10,... | collective-permute-start | bytes 294920 | tf_op jit(solution)/shard_map/ppermute | solution.py:28
  35.6 5.4 %collective-permute-start.5 = (f32[8,3,8,128]{3,2,1,0:T(8,128)S(1)}, f32[8,3,8,128]{3,2,1,0:T(8,128)S(1)}, u32[]{:S(2)}, u32[]{:S(2)}) collective-permute-start(f32[8,3,8,128]{3,2,1,0:T(8,128)S(1)} %get-tuple-element.44), channel_id=1, source_target_pairs={{0,1},{1,0},{2,3},{3,2},{4,5},{5,4},{6,7},{7,6},{8,9},{9,8},{10,11... | collective-permute-start | bytes 294920 | tf_op jit(solution)/shard_map/ppermute | solution.py:28

commit v5 on v4

--- a/solution.py
+++ b/solution.py
@@ -212,12 +212,11 @@
             row = rows[pl.ds(place if k == 0 else info_ref[k, y, r], 1), :]
             spread[lines, k * dof:(k + 1) * dof] = jnp.broadcast_to(row, (columns, dof))
 
-    block_rows = high.shape[1]
     pair = 2 * dof
     wide = 2 * pair
 
-    def solve_block(b, pairs):
-        lines = pl.ds(pl.multiple_of(b * block_rows, block_rows), block_rows)
+    def solve_block(lines, pairs):
+        inner = slice(0, lines.stop - lines.start)
         active = pairs * pair
         begin = start[lines, :]
         begin_high, begin_low = split(begin)
@@ -233,20 +232,20 @@
                 else:
                     source = (iteration - 1) % 2
                     image = (
-                        product(high[source, :, :active], high_ref[:active, lanes])
-                        + product(high[source, :, :active], low_ref[:active, lanes])
-                        + product(low[source, :, :active], high_ref[:active, lanes])
+                        product(high[source, inner, :active], high_ref[:active, lanes])
+                        + product(high[source, inner, :active], low_ref[:active, lanes])
+                        + product(low[source, inner, :active], high_ref[:active, lanes])
                     )
-                picture[:, lanes] = image
+                picture[inner, lanes] = image
                 first, second = split(spread[lines, lanes] * image)
-                weighted_high[:, lanes] = first
-                weighted_low[:, lanes] = second
+                weighted_high[inner, lanes] = first
+                weighted_low[inner, lanes] = second
             for base in range(0, active, pair):
                 lanes = slice(base, base + pair)
                 factor = spread[lines, lanes]
-                mean = product(weighted_high[:, lanes], ones)
-                mean = mean + product(weighted_low[:, lanes], ones)
-                change = jnp.where(factor > 0.0, picture[:, lanes] - factor * mean, 0.0)
+                mean = product(weighted_high[inner, lanes], ones)
+                mean = mean + product(weighted_low[inner, lanes], ones)
+                change = jnp.where(factor > 0.0, picture[inner, lanes] - factor * mean, 0.0)
                 result = -change if iteration == 0 else value[lines, lanes] - change
                 value[lines, lanes] = result
                 if iteration < ITERS - 1:
@@ -255,19 +254,17 @@
                             [result[:, :dof] + begin, result[:, dof:]], axis=1
                         )
                     first, second = split(result)
-                    high[iteration % 2, :, lanes] = first
-                    low[iteration % 2, :, lanes] = second
-
-    def solve_step(b, carry):
-        passed = b * (block_rows // columns)
-        pairs = jnp.int32(0)
-        for k in range(slots // 2):
-            pairs = pairs + jnp.where(longer[2 * k] > passed, 1, 0)
-        for k in range(1, slots // 2 + 1):
-            pl.when(pairs == k)(functools.partial(solve_block, b, k))
-        return carry
-
-    lax.fori_loop(0, spread.shape[0] // block_rows, solve_step, 0)
+                    high[iteration % 2, inner, lanes] = first
+                    low[iteration % 2, inner, lanes] = second
+
+    passed = high.shape[1] // columns
+    solve_block(slice(0, high.shape[1]), slots // 2)
+    pairs = jnp.int32(2)
+    for k in range(2, slots // 2):
+        pairs = pairs + jnp.where(longer[2 * k] > passed, 1, 0)
+    others = slice(high.shape[1], spread.shape[0])
+    for k in range(2, slots // 2 + 1):
+        pl.when(pairs == k)(functools.partial(solve_block, others, k))
 
     total[...] = jnp.zeros(total.shape, F32)
 
@@ -386,7 +383,7 @@
     whole = (row_count, col_count, columns, dof)
     side = shapes(row_count, REACH, columns, dof)
     total_rows = (row_count + 2 * REACH) * col_count * columns
-    block_rows = total_rows // 2
+    block_rows = 32 * columns
     own_sum, far_sum, near_sum, inverse = pl.pallas_call(
         functools.partial(
             solve_kernel, row_count=row_count, col_count=col_count, dof=dof, places=places

time: 41.9 us -> 41.5 us (level)
  the two profiles are of different devices: /device:TPU:193 before, /device:TPU:4 now
where the time goes in v5:
time: 41.5 us; the launch traced here: 41.2 us
  starting transfers between devices  22.3 us (54%)
  Pallas kernels  12.2 us (29%)
  waiting for transfers between devices  6.38 us (15%)
    ppermute x4, starting transfers between devices, swapped(): return lax.ppermute(value, axis, pairs)  14.4 us
    pallas_call x1, Pallas kernels, per_device(): pl.pallas_call(functools.partial(solve_kernel, row_count=row_count, col_c...  9.1 us
    ppermute x2, starting transfers between devices, moved(): return lax.ppermute(value, axis, pairs)  7.95 us
    ppermute x4, waiting for transfers between devices, swapped(): return lax.ppermute(value, axis, pairs)  4.59 us
    pallas_call x1, Pallas kernels, per_device(): pl.pallas_call(functools.partial(prepare_kernel, places=places), in_specs...  2.41 us
    ppermute x2, waiting for transfers between devices, moved(): return lax.ppermute(value, axis, pairs)  1.8 us
  transfers between devices with their start and end apart: 6, of which 3 were waited for; matrix products, arithmetic and copies ran while one was open for 0% of the time, Pallas kernels for 6%

profile of v5, /device:TPU:4, one launch (start us, length us, event | category | flops | bytes accessed | tf_op | source)
XLA Modules:
  0.0 41.2 jit_solution(611201207047708446)
XLA Ops:
  0.0 2.4 %collective-permute-start = (s32[8,4,128]{2,1,0:T(4,128)}, s32[8,4,128]{2,1,0:T(4,128)S(1)}, u32[]{:S(2)}, u32[]{:S(2)}) collective-permute-start(s32[8,4,128]{2,1,0:T(4,128)} %classes_ref.1), channel_id=1, source_target_pairs={{0,31},{1,2},{2,1},{3,4},{4,3},{5,6},{6,5},{7,8},{8,7},{9,10},{10,... | collective-permute-start | bytes 49160 | tf_op jit(solution)/shard_map/ppermute | solution.py:28
  2.4 4.1 %collective-permute-start.1 = (s32[8,4,128]{2,1,0:T(4,128)}, s32[8,4,128]{2,1,0:T(4,128)S(1)}, u32[]{:S(2)}, u32[]{:S(2)}) collective-permute-start(s32[8,4,128]{2,1,0:T(4,128)} %classes_ref.1), channel_id=1, source_target_pairs={{0,1},{1,0},{2,3},{3,2},{4,5},{5,4},{6,7},{7,6},{8,9},{9,8},{10,11... | collective-permute-start | bytes 49160 | tf_op jit(solution)/shard_map/ppermute | solution.py:28
  6.5 0.0 copy-start
  6.5 0.0 copy-start.1
  6.5 2.4 %prepare.1 = (s32[8,4,128]{2,1,0:T(4,128)S(1)}, s32[8,4,8]{2,1,0:T(4,128)S(1)}, s32[8,4,8]{2,1,0:T(4,128)S(1)}, s32[8,4,8]{2,1,0:T(4,128)S(1)}, bf16[1024,1024]{...) custom-call(s32[7,4,8]{2,1,0:T(4,128)} %bitcast.9, s32[7,4,8]{2,1,0:T(4,128)} %bitcast.10, s32[4,8]{1,0:T(4,128)} %bitcast.11, ...), custom_call_target="tpu_custom_call" | custom-call | flops 2097152 | bytes 8388608 | tf_op jit(solution)/shard_map/prepare/pallas_call | solution.py:344
  8.9 0.0 collective-permute-done.far_ref
  9.0 0.0 collective-permute-done.1.near_ref
  9.0 0.0 collective-permute-start.2
  9.0 7.9 %collective-permute-start.3 = (s32[26,4,128]{2,1,0:T(4,128)S(1)}, s32[26,4,128]{2,1,0:T(4,128)S(1)}, u32[]{:S(2)}, u32[]{:S(2)}) collective-permute-start(s32[26,4,128]{2,1,0:T(4,128)S(1)} %get-tuple-element.38), channel_id=1, source_target_pairs={{0,480},{32,0},{64,32},{96,64},{128,96},{160,128},{192,160},{224,1... | collective-permute-start | bytes 159752 | tf_op jit(solution)/shard_map/ppermute | solution.py:22
  17.0 1.8 %collective-permute-done.2.above_ref = s32[26,4,128]{2,1,0:T(4,128)S(1)} collective-permute-done((s32[26,4,128]{2,1,0:T(4,128)S(1)}, s32[26,4,128]{2,1,0:T(4,128)S(1)}, u32[]{:S(2)}, u32[]{:S(2)}) %collective-permute-start.2) | collective-permute-done | bytes 53280 | tf_op jit(solution)/shard_map/ppermute | solution.py:22
  18.8 0.1 slice.8
  18.8 0.0 collective-permute-done.3.below_ref
  18.8 0.1 pad_add_fusion.info_ref
  18.9 0.0 copy-done
  18.9 0.0 copy-done.1
  19.0 9.1 %solve.1 = (f32[8,4,8,128]{3,2,1,0:T(8,128)S(1)}, f32[8,3,8,128]{3,2,1,0:T(8,128)S(1)}, f32[8,3,8,128]{3,2,1,0:T(8,128)S(1)}, f32[8,4,128]{2,1,0:T(4,128)S(1)}) custom-call(s32[8,4,14]{2,1,0:T(4,128)S(1)} %pad_add_fusion.info_ref, f32[4]{0:T(128)S(1)} %copy-done.1, s32[32,128]{1,0:T(8,128)S(1)} %bitcast.7, s32[32,128]{1,0:T(8,128)S(1)} %bitcast.8, ...), custom_call_target="tpu_custom_call" | custom-call | tf_op jit(solution)/shard_map/solve/pallas_call | solution.py:387
  28.1 6.0 %collective-permute-start.4 = (f32[8,3,8,128]{3,2,1,0:T(8,128)S(1)}, f32[8,3,8,128]{3,2,1,0:T(8,128)S(1)}, u32[]{:S(2)}, u32[]{:S(2)}) collective-permute-start(f32[8,3,8,128]{3,2,1,0:T(8,128)S(1)} %get-tuple-element.43), channel_id=1, source_target_pairs={{0,31},{1,2},{2,1},{3,4},{4,3},{5,6},{6,5},{7,8},{8,7},{9,10},{10,... | collective-permute-start | bytes 294920 | tf_op jit(solution)/shard_map/ppermute | solution.py:28
  34.0 1.9 %collective-permute-start.5 = (f32[8,3,8,128]{3,2,1,0:T(8,128)S(1)}, f32[8,3,8,128]{3,2,1,0:T(8,128)S(1)}, u32[]{:S(2)}, u32[]{:S(2)}) collective-permute-start(f32[8,3,8,128]{3,2,1,0:T(8,128)S(1)} %get-tuple-element.44), channel_id=1, source_target_pairs={{0,1},{1,0},{2,3},{3,2},{4,5},{5,4},{6,7},{7,6},{8,9},{9,8},{10,11... | collective-permute-start | bytes 294920 | tf_op jit(solution)/shard_map/ppermute | solution.py:28
  35.9 0.7 %collective-permute-done.4.far_ref = f32[8,3,8,128]{3,2,1,0:T(8,128)S(1)} collective-permute-done((f32[8,3,8,128]{3,2,1,0:T(8,128)S(1)}, f32[8,3,8,128]{3,2,1,0:T(8,128)S(1)}, u32[]{:S(2)}, u32[]{:S(2)}) %collective-permute-start.4) | collective-permute-done | bytes 98336 | tf_op jit(solution)/shard_map/ppermute | solution.py:28
  36.6 3.9 %collective-permute-done.5.near_ref = f32[8,3,8,128]{3,2,1,0:T(8,128)S(1)} collective-permute-done((f32[8,3,8,128]{3,2,1,0:T(8,128)S(1)}, f32[8,3,8,128]{3,2,1,0:T(8,128)S(1)}, u32[]{:S(2)}, u32[]{:S(2)}) %collective-permute-start.5) | collective-permute-done | bytes 98336 | tf_op jit(solution)/shard_map/ppermute | solution.py:28
  40.5 0.7 %final.1 = f32[8,4,8,128]{3,2,1,0:T(8,128)} custom-call(f32[8,4,128]{2,1,0:T(4,128)S(1)} %get-tuple-element.41.inverse_ref, f32[8,4,8,128]{3,2,1,0:T(8,128)S(1)} %get-tuple-element.42.own_ref, f32[8,3,8,128]{3,2,1,0:T(8,128)S(1)} %collective-permute-done.4.far_ref, f32[8,3,8,128]{3,2,1,0:T(8,128)S(1)} %collective-permute-done.5.near_ref), custom_call_target="tpu_custom_call" | custom-call | tf_op jit(solution)/shard_map/final/pallas_call | solution.py:416
  (2 shorter events, 0.0 us)
Async XLA Ops:
  0.0 9.0 %collective-permute-start = (s32[8,4,128]{2,1,0:T(4,128)}, s32[8,4,128]{2,1,0:T(4,128)S(1)}, u32[]{:S(2)}, u32[]{:S(2)}) collective-permute-start(s32[8,4,128]{2,1,0:T(4,128)} %classes_ref.1), channel_id=1, source_target_pairs={{0,31},{1,2},{2,1},{3,4},{4,3},{5,6},{6,5},{7,8},{8,7},{9,10},{10,... | collective-permute-start | bytes 49160 | tf_op jit(solution)/shard_map/ppermute | solution.py:28
  2.4 6.5 %collective-permute-start.1 = (s32[8,4,128]{2,1,0:T(4,128)}, s32[8,4,128]{2,1,0:T(4,128)S(1)}, u32[]{:S(2)}, u32[]{:S(2)}) collective-permute-start(s32[8,4,128]{2,1,0:T(4,128)} %classes_ref.1), channel_id=1, source_target_pairs={{0,1},{1,0},{2,3},{3,2},{4,5},{5,4},{6,7},{7,6},{8,9},{9,8},{10,11... | collective-permute-start | bytes 49160 | tf_op jit(solution)/shard_map/ppermute | solution.py:28
  6.5 12.4 %copy-start = (f32[8,128]{1,0:T(8,128)S(1)}, f32[8,128]{1,0:T(8,128)}, u32[]{:S(2)}) copy-start(f32[8,128]{1,0:T(8,128)} %coarse_ref.1) | copy-start | bytes 12292
  6.5 12.4 %copy-start.1 = (f32[4]{0:T(128)S(1)}, f32[4]{0:T(128)}, u32[]{:S(2)}) copy-start(f32[4]{0:T(128)} %contrast_ref.1) | copy-start | bytes 52
  9.0 9.8 %collective-permute-start.2 = (s32[26,4,128]{2,1,0:T(4,128)S(1)}, s32[26,4,128]{2,1,0:T(4,128)S(1)}, u32[]{:S(2)}, u32[]{:S(2)}) collective-permute-start(s32[26,4,128]{2,1,0:T(4,128)S(1)} %get-tuple-element.36), channel_id=1, source_target_pairs={{0,32},{32,64},{64,96},{96,128},{128,160},{160,192},{192,224},{224... | collective-permute-start | bytes 159752 | tf_op jit(solution)/shard_map/ppermute | solution.py:22
  9.0 9.8 %collective-permute-start.3 = (s32[26,4,128]{2,1,0:T(4,128)S(1)}, s32[26,4,128]{2,1,0:T(4,128)S(1)}, u32[]{:S(2)}, u32[]{:S(2)}) collective-permute-start(s32[26,4,128]{2,1,0:T(4,128)S(1)} %get-tuple-element.38), channel_id=1, source_target_pairs={{0,480},{32,0},{64,32},{96,64},{128,96},{160,128},{192,160},{224,1... | collective-permute-start | bytes 159752 | tf_op jit(solution)/shard_map/ppermute | solution.py:22
  28.1 8.5 %collective-permute-start.4 = (f32[8,3,8,128]{3,2,1,0:T(8,128)S(1)}, f32[8,3,8,128]{3,2,1,0:T(8,128)S(1)}, u32[]{:S(2)}, u32[]{:S(2)}) collective-permute-start(f32[8,3,8,128]{3,2,1,0:T(8,128)S(1)} %get-tuple-element.43), channel_id=1, source_target_pairs={{0,31},{1,2},{2,1},{3,4},{4,3},{5,6},{6,5},{7,8},{8,7},{9,10},{10,... | collective-permute-start | bytes 294920 | tf_op jit(solution)/shard_map/ppermute | solution.py:28
  34.0 6.5 %collective-permute-start.5 = (f32[8,3,8,128]{3,2,1,0:T(8,128)S(1)}, f32[8,3,8,128]{3,2,1,0:T(8,128)S(1)}, u32[]{:S(2)}, u32[]{:S(2)}) collective-permute-start(f32[8,3,8,128]{3,2,1,0:T(8,128)S(1)} %get-tuple-element.44), channel_id=1, source_target_pairs={{0,1},{1,0},{2,3},{3,2},{4,5},{5,4},{6,7},{7,6},{8,9},{9,8},{10,11... | collective-permute-start | bytes 294920 | tf_op jit(solution)/shard_map/ppermute | solution.py:28
